TPU v7x, 32 devices: a whole 2x2x4 slice. The times are simulated.
32 devices in a mesh: tensor: 4 (over z), inner: 4 (over x, core), outer: 2 (over y).
Axes of the slice: x: 2, y: 2, z: 4, core: 2. Of those that a mesh axis runs over, the one named last changes fastest.
Arguments:
- tokens: bfloat16 [64, 261, 768], P(('inner', 'outer')), may hold values from -6 to 6
- patch_mask: int32 [64, 256], P(('inner', 'outer')), may hold values from 0 to 1, as said below
- cotangent: bfloat16 [64, 261, 768], P(('inner', 'outer')), may hold values from -6 to 6
- mask_token: float32 [768], replicated, may hold values from -5 to 5
- pos_embed: float32 [261, 768], replicated, may hold values from -2.5 to 2.5
- pre_attn_gain: float32 [768], replicated, may hold values from 0.25 to 1.75
- pre_attn_bias: float32 [768], replicated, may hold values from -1.5 to 1.5
- qkv_weight: bfloat16 [768, 3, 768], P(None, None, 'tensor'), may hold values from -0.21875 to 0.21875
- qv_bias: float32 [2, 768], P(None, 'tensor'), may hold values from -2.5 to 2.5
- proj_weight: bfloat16 [768, 768], P('tensor'), may hold values from -0.875 to 0.875
- proj_bias: float32 [768], replicated, may hold values from -1.5 to 1.5
- attn_scale: float32 [768], replicated, may hold values from 0.5 to 1.5
- pre_mlp_gain: float32 [768], replicated, may hold values from 0.25 to 1.75
- pre_mlp_bias: float32 [768], replicated, may hold values from -1.5 to 1.5
- fc1_weight: bfloat16 [768, 3072], P(None, 'tensor'), may hold values from -0.21875 to 0.21875
- fc1_bias: float32 [3072], P('tensor'), may hold values from -2.5 to 2.5
- fc2_weight: bfloat16 [3072, 768], P('tensor'), may hold values from -0.21875 to 0.21875
- fc2_bias: float32 [768], replicated, may hold values from -1.5 to 1.5
- mlp_scale: float32 [768], replicated, may hold values from 0.5 to 1.5
Outputs:
- result: bfloat16 [64, 261, 768], P(('inner', 'outer'))
- grad_tokens: float32 [64, 261, 768], P(('inner', 'outer'))
- grad_mask_token: float32 [768], P('inner')
- grad_pos_embed: float32 [261, 768], P(None, 'inner')
- grad_pre_attn_gain: float32 [768], P('inner')
- grad_pre_attn_bias: float32 [768], P('inner')
- grad_qkv_weight: float32 [768, 3, 768], P('inner', None, 'tensor')
- grad_qv_bias: float32 [2, 768], P(None, ('tensor', 'inner'))
- grad_proj_weight: float32 [768, 768], P('tensor', 'inner')
- grad_proj_bias: float32 [768], P('inner')
- grad_attn_scale: float32 [768], P('inner')
- grad_pre_mlp_gain: float32 [768], P('inner')
- grad_pre_mlp_bias: float32 [768], P('inner')
- grad_fc1_weight: float32 [768, 3072], P('inner', 'tensor')
- grad_fc1_bias: float32 [3072], P(('tensor', 'inner'))
- grad_fc2_weight: float32 [3072, 768], P('tensor', 'inner')
- grad_fc2_bias: float32 [768], P('inner')
- grad_mlp_scale: float32 [768], P('inner')
Inputs may be any that keep to these rules, and one draw needn't show every extreme that they name: `patch_mask`: in each crop the ones form one axis-aligned rectangle of the row-major 16 x 16 patch grid, covering at most half of its patches.
All inputs are finite; a program needn't handle non-finite values.
Results may differ from a plain program's by a relative error of at most 0.012.
The roundings to bfloat16 on the way count: a program that leaves them out, or rounds other values in their place, can miss the bound.
Values sent between devices are 32-bit elements; how exact they have to be, the bound alone decides.
No kernel may reach another device: no remote copies, remote signals or barrier semaphores. Data moves between devices by JAX's collectives and lax.ppermute only.
A program may use at most 192 MiB of HBM per device.

v0:
```python
import jax
import jax.numpy as jnp
from jax import lax
from jax.sharding import PartitionSpec as P

HEAD_DIM = 64


EPS = 1e-06


def layer_norm(field, gain_vec, bias_vec):
    center = field - jnp.mean(field, -1, keepdims=True)
    spread = jnp.mean(center * center, -1, keepdims=True)
    return center * lax.rsqrt(spread + EPS) * gain_vec + bias_vec


def gelu_exact(field):
    return jax.nn.gelu(field, approximate=False)


def per_device(
    tokens,
    patch_mask,
    cotangent,
    mask_token,
    pos_embed,
    pre_attn_gain,
    pre_attn_bias,
    qkv_weight,
    qv_bias,
    proj_weight,
    proj_bias,
    attn_scale,
    pre_mlp_gain,
    pre_mlp_bias,
    fc1_weight,
    fc1_bias,
    fc2_weight,
    fc2_bias,
    mlp_scale,
):
    crop_count, seq_length, model_width = tokens.shape
    row_count = crop_count * seq_length
    head_width = qkv_weight.shape[2]
    head_count = head_width // HEAD_DIM
    factor = HEAD_DIM ** (-0.5)
    prefix_zeros = jnp.zeros((crop_count, seq_length - patch_mask.shape[1]), jnp.int32)
    flagged = (jnp.concatenate([prefix_zeros, patch_mask], 1) == 1)[:, :, None]
    begin = (jnp.where(flagged, mask_token, tokens.astype(jnp.float32)) + pos_embed).reshape(
        row_count, model_width
    )
    normed, attn_norm_back = jax.vjp(layer_norm, begin, pre_attn_gain, pre_attn_bias)
    normed_low = normed.astype(jnp.bfloat16)
    bias_rows = jnp.stack([qv_bias[0], jnp.zeros_like(qv_bias[0]), qv_bias[1]])
    mixed = (
        jnp.einsum("rd,dtj->rtj", normed_low, qkv_weight, preferred_element_type=jnp.float32)
        + bias_rows
    )
    mixed_low = mixed.astype(jnp.bfloat16).reshape(crop_count, seq_length, 3, head_count, HEAD_DIM)
    query_low = mixed_low[:, :, 0]
    keys_low = mixed_low[:, :, 1]
    values_low = mixed_low[:, :, 2]
    scores = (
        jnp.einsum("cqhe,ckhe->chqk", query_low, keys_low, preferred_element_type=jnp.float32)
        * factor
    )
    row_max = jnp.max(scores, -1, keepdims=True)
    shifted = jnp.exp(scores - row_max)
    row_sum = jnp.sum(shifted, -1, keepdims=True)
    log_total = row_max + jnp.log(row_sum)
    probs_low = (shifted / row_sum).astype(jnp.bfloat16)
    attended_low = (
        jnp.einsum("chqk,ckhe->cqhe", probs_low, values_low, preferred_element_type=jnp.float32)
        .astype(jnp.bfloat16)
        .reshape(row_count, head_width)
    )
    branch = (
        lax.psum(jnp.dot(attended_low, proj_weight, preferred_element_type=jnp.float32), "tensor")
        + proj_bias
    )
    middle = begin + attn_scale * branch
    normed_mlp, mlp_norm_back = jax.vjp(layer_norm, middle, pre_mlp_gain, pre_mlp_bias)
    normed_mlp_low = normed_mlp.astype(jnp.bfloat16)
    hidden = jnp.dot(normed_mlp_low, fc1_weight, preferred_element_type=jnp.float32) + fc1_bias
    activated, gelu_back = jax.vjp(gelu_exact, hidden)
    activated_low = activated.astype(jnp.bfloat16)
    output = (
        lax.psum(jnp.dot(activated_low, fc2_weight, preferred_element_type=jnp.float32), "tensor")
        + fc2_bias
    )
    result = (
        (middle + mlp_scale * output)
        .astype(jnp.bfloat16)
        .reshape(crop_count, seq_length, model_width)
    )
    upstream = cotangent.astype(jnp.float32).reshape(row_count, model_width)
    grad_mlp_scale = jnp.sum(upstream * output, 0)
    grad_output = upstream * mlp_scale
    grad_fc2_bias = jnp.sum(grad_output, 0)
    grad_output_low = grad_output.astype(jnp.bfloat16)
    grad_fc2_weight = jnp.einsum(
        "rf,rd->fd", activated_low, grad_output_low, preferred_element_type=jnp.float32
    )
    grad_activated = jnp.einsum(
        "rd,fd->rf", grad_output_low, fc2_weight, preferred_element_type=jnp.float32
    )
    grad_hidden = gelu_back(grad_activated)[0]
    grad_fc1_bias = jnp.sum(grad_hidden, 0)
    grad_hidden_low = grad_hidden.astype(jnp.bfloat16)
    grad_fc1_weight = jnp.einsum(
        "rd,rf->df", normed_mlp_low, grad_hidden_low, preferred_element_type=jnp.float32
    )
    grad_normed_mlp = lax.psum(
        jnp.einsum("rf,df->rd", grad_hidden_low, fc1_weight, preferred_element_type=jnp.float32),
        "tensor",
    )
    grad_mid_part, grad_mlp_gain, grad_mlp_bias = mlp_norm_back(grad_normed_mlp)
    grad_middle = upstream + grad_mid_part
    grad_attn_scale = jnp.sum(grad_middle * branch, 0)
    grad_branch = grad_middle * attn_scale
    grad_proj_bias = jnp.sum(grad_branch, 0)
    grad_branch_low = grad_branch.astype(jnp.bfloat16)
    grad_proj_weight = jnp.einsum(
        "rj,rd->jd", attended_low, grad_branch_low, preferred_element_type=jnp.float32
    )
    grad_attended = jnp.einsum(
        "rd,jd->rj", grad_branch_low, proj_weight, preferred_element_type=jnp.float32
    )
    grad_attended = grad_attended.astype(jnp.bfloat16).reshape(
        crop_count, seq_length, head_count, HEAD_DIM
    )
    scores_again = (
        jnp.einsum("cqhe,ckhe->chqk", query_low, keys_low, preferred_element_type=jnp.float32)
        * factor
    )
    probs_again = jnp.exp(scores_again - log_total)
    probs_again_low = probs_again.astype(jnp.bfloat16)
    grad_values = jnp.einsum(
        "chqk,cqhe->ckhe", probs_again_low, grad_attended, preferred_element_type=jnp.float32
    )
    grad_probs = jnp.einsum(
        "cqhe,ckhe->chqk", grad_attended, values_low, preferred_element_type=jnp.float32
    )
    grad_scores = probs_again * (grad_probs - jnp.sum(grad_probs * probs_again, -1, keepdims=True))
    grad_scores_low = grad_scores.astype(jnp.bfloat16)
    grad_query = (
        jnp.einsum("chqk,ckhe->cqhe", grad_scores_low, keys_low, preferred_element_type=jnp.float32)
        * factor
    )
    grad_keys = (
        jnp.einsum(
            "chqk,cqhe->ckhe", grad_scores_low, query_low, preferred_element_type=jnp.float32
        )
        * factor
    )
    grad_mixed = jnp.stack([grad_query, grad_keys, grad_values], 2).reshape(
        row_count, 3, head_width
    )
    grad_qv_bias = jnp.stack([jnp.sum(grad_mixed[:, 0], 0), jnp.sum(grad_mixed[:, 2], 0)])
    grad_mixed_low = grad_mixed.astype(jnp.bfloat16)
    grad_qkv_weight = jnp.einsum(
        "rd,rtj->dtj", normed_low, grad_mixed_low, preferred_element_type=jnp.float32
    )
    grad_normed = lax.psum(
        jnp.einsum("rtj,dtj->rd", grad_mixed_low, qkv_weight, preferred_element_type=jnp.float32),
        "tensor",
    )
    grad_begin_part, grad_attn_gain, grad_attn_bias = attn_norm_back(grad_normed)
    grad_begin = (grad_middle + grad_begin_part).reshape(crop_count, seq_length, model_width)
    grad_tokens = jnp.where(flagged, 0.0, grad_begin)
    grad_mask_token = jnp.sum(jnp.where(flagged, grad_begin, 0.0), (0, 1))
    grad_pos_embed = jnp.sum(grad_begin, 0)
    shares = (
        lax.psum_scatter(grad_mask_token, "inner", scatter_dimension=0, tiled=True),
        lax.psum_scatter(grad_pos_embed, "inner", scatter_dimension=1, tiled=True),
        lax.psum_scatter(grad_attn_gain, "inner", scatter_dimension=0, tiled=True),
        lax.psum_scatter(grad_attn_bias, "inner", scatter_dimension=0, tiled=True),
        lax.psum_scatter(grad_qkv_weight, "inner", scatter_dimension=0, tiled=True),
        lax.psum_scatter(grad_qv_bias, "inner", scatter_dimension=1, tiled=True),
        lax.psum_scatter(grad_proj_weight, "inner", scatter_dimension=1, tiled=True),
        lax.psum_scatter(grad_proj_bias, "inner", scatter_dimension=0, tiled=True),
        lax.psum_scatter(grad_attn_scale, "inner", scatter_dimension=0, tiled=True),
        lax.psum_scatter(grad_mlp_gain, "inner", scatter_dimension=0, tiled=True),
        lax.psum_scatter(grad_mlp_bias, "inner", scatter_dimension=0, tiled=True),
        lax.psum_scatter(grad_fc1_weight, "inner", scatter_dimension=0, tiled=True),
        lax.psum_scatter(grad_fc1_bias, "inner", scatter_dimension=0, tiled=True),
        lax.psum_scatter(grad_fc2_weight, "inner", scatter_dimension=1, tiled=True),
        lax.psum_scatter(grad_fc2_bias, "inner", scatter_dimension=0, tiled=True),
        lax.psum_scatter(grad_mlp_scale, "inner", scatter_dimension=0, tiled=True),
    )
    summed = lax.psum(
        (
            shares[0],
            shares[1],
            shares[2],
            shares[3],
            shares[4],
            shares[5],
            shares[6],
            shares[7],
            shares[8],
            shares[9],
            shares[10],
            shares[11],
            shares[12],
            shares[13],
            shares[14],
            shares[15],
        ),
        "outer",
    )
    return (
        result,
        grad_tokens,
        summed[0],
        summed[1],
        summed[2],
        summed[3],
        summed[4],
        summed[5],
        summed[6],
        summed[7],
        summed[8],
        summed[9],
        summed[10],
        summed[11],
        summed[12],
        summed[13],
        summed[14],
        summed[15],
    )


def solution(mesh):
    in_specs = (
        P(("inner", "outer"), None, None),
        P(("inner", "outer"), None),
        P(("inner", "outer"), None, None),
        P(),
        P(),
        P(),
        P(),
        P(None, None, "tensor"),
        P(None, "tensor"),
        P("tensor", None),
        P(),
        P(),
        P(),
        P(),
        P(None, "tensor"),
        P("tensor"),
        P("tensor", None),
        P(),
        P(),
    )
    out_specs = (
        P(("inner", "outer"), None, None),
        P(("inner", "outer"), None, None),
        P("inner"),
        P(None, "inner"),
        P("inner"),
        P("inner"),
        P("inner", None, "tensor"),
        P(None, ("tensor", "inner")),
        P("tensor", "inner"),
        P("inner"),
        P("inner"),
        P("inner"),
        P("inner"),
        P("inner", "tensor"),
        P(("tensor", "inner")),
        P("tensor", "inner"),
        P("inner"),
        P("inner"),
    )
    return jax.shard_map(
        per_device, mesh=mesh, in_specs=in_specs, out_specs=out_specs, check_vma=False
    )
```

profile of v0, /device:TPU:0, one launch (start us, length us, event | category | flops | bytes accessed | tf_op | source)
XLA Modules:
  0.0 1338.6 jit_solution(14352750679543017473)
XLA Ops:
  8.1 3.5 fusion.29
  11.8 7.3 multiply_reduce_fusion.2
  19.2 6.3 reshape.178
  25.7 3.6 add_convert_fusion.2
  33.5 7.2 reshape.179
  46.8 2.9 fusion.20
  51.3 3.8 fusion.42
  55.2 5.2 copy.74
  60.4 6.4 reshape.182
  66.8 218.1 %all-reduce.20.cloned.1.call-done = f32[2088,768]{1,0:T(8,128)} async-done(((f32[2088,768]{1,0:T(8,128)}), f32[2088,768]{1,0:T(8,128)}) %all-reduce.20.cloned.1.call-update) | async-done | bytes 6414352 | tf_op jit(solution)/shard_map/psum | solution.py:79
  284.9 5.7 fusion.36
  291.7 18.6 %multiply_convert_fusion.2 = (bf16[2088,768]{1,0:T(8,128)(2,1)}, f32[2088,768]{1,0:T(8,128)}, f32[2088,768]{1,0:T(8,128)}) fusion(f32[768]{0:T(1024)S(1)} %copy-done.50, bf16[768,768]{1,0:T(8,128)(2,1)S(1)} %copy-done, f32[2088,768]{1,0:T(8,128)S(1)} %get-tuple-element.118, f32[768]{0:T(1024)S(1)} %copy-done.51, f32[768]{0:T(1024)S(1)} %copy-done.39, ...), kind=kOutput, calls=%fused_computation.26 | convolution fusion | flops 2576959488 | bytes 23655744 | tf_op jit(solution)/shard_map/dot_general | solution.py:85
  310.3 8.2 fusion.40
  320.2 4.7 fusion.17
  325.6 7.3 fusion.43
  333.0 217.9 %all-reduce.22.cloned.1.call-done = f32[2088,768]{1,0:T(8,128)} async-done(((f32[2088,768]{1,0:T(8,128)}), f32[2088,768]{1,0:T(8,128)}) %all-reduce.22.cloned.1.call-update) | async-done | bytes 6414352 | tf_op jit(solution)/shard_map/psum | solution.py:114
  550.8 6.6 multiply_reduce_fusion.5
  557.5 9.5 fusion.34
  567.1 6.3 multiply_reduce_fusion.6
  573.4 2.6 copy-done.4
  578.8 7.6 bitcast_convert_fusion
  586.4 7.8 multiply_reduce_fusion
  594.3 10.9 multiply_convert_fusion
  605.2 4.5 fusion.21
  609.7 2.7 bitcast_convert_fusion.1
  622.0 6.7 convolution_bitcast_fusion
  629.9 5.3 convolution_bitcast_fusion.1
  635.3 427.5 %all-reduce.24.cloned.1.call-done = (f32[2088,768]{1,0:T(8,128)}, f32[2088,768]{1,0:T(8,128)}) async-done(((f32[2088,768]{1,0:T(8,128)}, f32[2088,768]{1,0:T(8,128)}), (f32[2088,768]{1,0:T(8,128)}, f32[2088,768]{1,0:T(8,128)})) %all-reduce.24.cloned.1.call-update) | async-done | bytes 12828688 | tf_op jit(solution)/shard_map/psum | solution.py:89
  1062.8 6.1 multiply_reduce_fusion.7
  1068.9 7.6 fusion.33
  1076.5 7.8 select_reduce_fusion
  1084.4 6.3 reshape.184
  1090.7 5.0 fusion.37
  1097.3 8.8 fusion.15
  1106.3 8.2 fusion.22
  1114.6 7.2 fusion.13
  1128.6 28.4 %reduce-scatter.15.cloned.1.call-done = f32[192,768]{1,0:T(8,128)} async-done(((f32[768,768]{1,0:T(8,128)}), f32[192,768]{1,0:T(8,128)}) %reduce-scatter.15.cloned.1.call-update) | async-done | bytes 589840 | tf_op jit(solution)/shard_map/reduce_scatter | solution.py:186
  1157.0 35.8 %reduce-scatter.17.cloned.1.call-done = f32[768,192]{0,1:T(8,128)} async-done(((f32[768,768]{0,1:T(8,128)}), f32[768,192]{0,1:T(8,128)}) %reduce-scatter.17.cloned.1.call-update) | async-done | bytes 589840 | tf_op jit(solution)/shard_map/reduce_scatter | solution.py:188
  1192.8 36.2 %reduce-scatter.13.cloned.1.call-done = f32[192,3,192]{2,0,1:T(8,128)} async-done(((f32[768,3,192]{2,0,1:T(8,128)}), f32[192,3,192]{2,0,1:T(8,128)}) %reduce-scatter.13.cloned.1.call-update) | async-done | bytes 442384 | tf_op jit(solution)/shard_map/reduce_scatter | solution.py:179
  1230.3 2.6 multiply_reduce_fusion.4
  1232.9 18.8 %reduce-scatter.21.cloned.1.call-done = f32[48,2]{1,0:T(8,128)} async-done(((f32[192,2]{1,0:T(8,128)}), f32[48,2]{1,0:T(8,128)}) %reduce-scatter.21.cloned.1.call-update) | async-done | bytes 400
  1252.6 9.5 multiply_reduce_fusion.3
  1262.2 11.6 all-reduce.11
  1274.5 4.5 reshape.181
  1279.0 4.2 copy.83
  1283.3 7.7 copy.84
  1291.0 8.9 all-reduce.13
  1299.9 22.4 %all-reduce.26.cloned.1.call-done = (f32[261,192]{1,0:T(8,128)}, f32[192,3,192]{2,0,1:T(8,128)}, f32[192,192]{1,0:T(8,128)}, f32[192,768]{1,0:T(8,128)}, f32[768,192]{0,1:T(8,128)}) async-done(((f32[261,192]{1,0:T(8,128)}, f32[192,3,192]{2,0,1:T(8,128)}, f32[192,192]{1,0:T(8,128)}, f32[192,768]{1,0:T(8,128)}, f32[768,192]{0,1:T(8,128)}), (f32[261,192]{1,0:T(8,128)}, f32[192,3,192]{2,0,1:T(8,128)}, ...) | async-done | bytes 1969936 | tf_op jit(solution)/shard_map/psum | solution.py:192
  (208 shorter events, 49.8 us)
Async XLA Ops:
  7.2 284.4 %copy-start = (bf16[768,768]{1,0:T(8,128)(2,1)S(1)}, bf16[768,768]{1,0:T(8,128)(2,1)}, u32[]{:S(2)}) copy-start(bf16[768,768]{1,0:T(8,128)(2,1)} %param.33) | copy-start | bytes 3538948
  7.2 277.7 %all-reduce.20.cloned.1.call-start = ((), (), s32[]{:S(2)}) async-start(), calls=%async_computation.6 | async-start | bytes 12828672 | tf_op jit(solution)/shard_map/psum | solution.py:79
  8.1 10.9 copy-start.31
  8.1 11.0 copy-start.47
  11.8 13.9 %copy-start.20 = (f32[2088]{0:T(1024)}, f32[2088]{0:T(1024)S(1)}, u32[]{:S(2)}) copy-start(f32[2088]{0:T(1024)S(1)} %div.47) | copy-start | bytes 25060
  19.2 6.4 copy-start.28
  19.2 6.5 copy-start.22
  19.2 6.5 copy-start.33
  19.2 6.5 copy-start.44
  55.2 495.7 %all-reduce.22.cloned.1.call-start = ((), (), s32[]{:S(2)}) async-start(), calls=%async_computation.7 | async-start | bytes 12828672 | tf_op jit(solution)/shard_map/psum | solution.py:114
  60.4 224.5 %copy-start.30 = (f32[768]{0:T(1024)S(1)}, f32[768]{0:T(1024)}, u32[]{:S(2)}) copy-start(f32[768]{0:T(1024)} %param.30) | copy-start | bytes 9220
  60.4 224.5 %copy-start.43 = (f32[768]{0:T(1024)S(1)}, f32[768]{0:T(1024)}, u32[]{:S(2)}) copy-start(f32[768]{0:T(1024)} %param.29) | copy-start | bytes 9220
  290.6 19.7 %copy-start.3 = (f32[2088,768]{1,0:T(8,128)}, f32[2088,768]{1,0:T(8,128)S(1)}, u32[]{:S(2)}) copy-start(f32[2088,768]{1,0:T(8,128)S(1)} %get-tuple-element.118) | copy-start | bytes 19243012
  290.7 19.6 %slice-start.2 = ((s8[6414336]{0:T(1024)(128)(4,1)}), s8[4194304]{0:T(1024)(128)(4,1)S(1)}, s32[]{:S(2)}) async-start(s8[6414336]{0:T(1024)(128)(4,1)} %bitcast.87), calls=%async_computation.18 | async-start | bytes 8388608
  291.6 265.9 %copy-start.26 = (f32[2088]{0:T(1024)}, f32[2088]{0:T(1024)S(1)}, u32[]{:S(2)}) copy-start(f32[2088]{0:T(1024)S(1)} %fusion.30) | copy-start | bytes 25060
  291.6 18.7 %slice-start.3 = ((s8[6414336]{0:T(1024)(128)(4,1)}), s8[2220032]{0:T(1024)(128)(4,1)S(1)}, s32[]{:S(2)}) async-start(s8[6414336]{0:T(1024)(128)(4,1)} %bitcast.87), calls=%async_computation.19 | async-start | bytes 4440064
  291.6 18.6 %copy-start.37 = (f32[768]{0:T(1024)S(1)}, f32[768]{0:T(1024)}, u32[]{:S(2)}) copy-start(f32[768]{0:T(1024)} %param.37) | copy-start | bytes 9220
  291.7 18.6 %copy-start.48 = (bf16[768,768]{1,0:T(8,128)(2,1)S(1)}, bf16[768,768]{1,0:T(8,128)(2,1)}, u32[]{:S(2)}) copy-start(bf16[768,768]{1,0:T(8,128)(2,1)} %param.35) | copy-start | bytes 3538948
  324.8 737.9 %all-reduce.24.cloned.1.call-start = ((), (), s32[]{:S(2)}) async-start(), calls=%async_computation.14 | async-start | bytes 25657344 | tf_op jit(solution)/shard_map/psum | solution.py:89
  550.8 16.2 %slice-start.4 = ((s8[6414336]{0:T(1024)(128)(4,1)}), s8[4194304]{0:T(1024)(128)(4,1)S(1)}, s32[]{:S(2)}) async-start(s8[6414336]{0:T(1024)(128)(4,1)} %bitcast.89), calls=%async_computation.20 | async-start | bytes 8388608
  557.5 9.5 slice-start.5
  578.8 7.7 copy-start.15
  594.3 10.9 copy-start.9
  628.8 434.0 %copy-start.21 = (f32[2088]{0:T(1024)S(1)}, f32[2088]{0:T(1024)}, u32[]{:S(2)}) copy-start(f32[2088]{0:T(1024)} %copy-done.20) | copy-start | bytes 25060
  628.8 434.0 %copy-start.23 = (f32[2088]{0:T(1024)S(1)}, f32[2088]{0:T(1024)}, u32[]{:S(2)}) copy-start(f32[2088]{0:T(1024)} %copy-done.22) | copy-start | bytes 25060
  628.8 434.0 %copy-start.34 = (f32[768]{0:T(1024)S(1)}, f32[768]{0:T(1024)}, u32[]{:S(2)}) copy-start(f32[768]{0:T(1024)} %param.24) | copy-start | bytes 9220
  628.8 496.3 %reduce-scatter.23.cloned.1.call-start = ((), (), s32[]{:S(2)}) async-start(), calls=%async_computation.13 | async-start | bytes 983040
  629.9 439.0 %slice-start = ((s8[6414336]{0:T(1024)(128)(4,1)}), s8[2220032]{0:T(1024)(128)(4,1)S(1)}, s32[]{:S(2)}) async-start(s8[6414336]{0:T(1024)(128)(4,1)} %bitcast.85), calls=%async_computation.16 | async-start | bytes 4440064
  635.2 491.6 %reduce-scatter.19.cloned.1.call-start = ((), (), s32[]{:S(2)}) async-start(), calls=%async_computation.11 | async-start | bytes 1474560
  1062.8 6.1 slice-start.1
  1090.7 6.5 copy-start.27
  1090.7 6.5 copy-start.40
  1090.7 6.5 copy-start.52
  1097.2 9.2 copy-start.38
  1097.2 59.8 %reduce-scatter.15.cloned.1.call-start = ((), (), s32[]{:S(2)}) async-start(), calls=%async_computation.9 | async-start | bytes 2949120 | tf_op jit(solution)/shard_map/reduce_scatter | solution.py:186
  1106.1 86.7 %reduce-scatter.17.cloned.1.call-start = ((), (), s32[]{:S(2)}) async-start(), calls=%async_computation.10 | async-start | bytes 2949120 | tf_op jit(solution)/shard_map/reduce_scatter | solution.py:188
  1114.5 9.3 copy-start.10
  1114.5 114.5 %reduce-scatter.13.cloned.1.call-start = ((), (), s32[]{:S(2)}) async-start(), calls=%async_computation.8 | async-start | bytes 2949120 | tf_op jit(solution)/shard_map/reduce_scatter | solution.py:179
  1121.8 107.2 %copy-start.53 = (u32[32]{0:T(128)S(1)}, u32[32]{0:T(128)}, u32[]{:S(2)}) copy-start(u32[32]{0:T(128)} %constant.91) | copy-start | bytes 388
  1121.8 130.7 %copy-start.45 = (f32[768]{0:T(1024)S(1)}, f32[768]{0:T(1024)}, u32[]{:S(2)}) copy-start(f32[768]{0:T(1024)} %param.36) | copy-start | bytes 9220
  1121.8 129.9 %reduce-scatter.21.cloned.1.call-start = ((), (), s32[]{:S(2)}) async-start(), calls=%async_computation.12 | async-start | bytes 122880
  1125.0 197.3 %all-reduce.26.cloned.1.call-start = ((), (), s32[]{:S(2)}) async-start(), calls=%async_computation.15 | async-start | bytes 4472832 | tf_op jit(solution)/shard_map/psum | solution.py:192
  1252.5 9.6 copy-start.35
  1252.5 9.6 copy-start.36
  1252.5 9.6 copy-start.41
  1252.6 9.6 copy-start.42
  1252.6 9.6 copy-start.46
  1283.3 48.1 %copy-start.1 = (bf16[768,768]{1,0:T(8,128)(2,1)S(1)}, bf16[768,768]{1,0:T(8,128)(2,1)}, u32[]{:S(2)}) copy-start(bf16[768,768]{1,0:T(8,128)(2,1)} %param.33) | copy-start | bytes 3538948
  (23 other events, 63.5 us)
Sparse Core Ops, SparseCore 0:
  55.3 229.6 all-reduce.19
  325.0 225.8 all-reduce.21
  628.9 433.8 all-reduce.23
  1065.2 22.2 reduce-scatter.22
  1097.3 24.1 reduce-scatter.18
  1123.9 33.0 reduce-scatter.14
  1159.7 33.0 reduce-scatter.16
  1195.9 33.0 reduce-scatter.12
  1232.2 19.5 reduce-scatter.20
  1255.5 66.7 all-reduce.25
where the time goes:
time: 1350 us; the launch traced here: 1340 us
  waiting for transfers between devices  1010 us (75%)
  matrix products  110 us (8%)
  other arithmetic  99.8 us (7%)
  local copies, waits for them, and re-layouts  86.2 us (6%)
  blocking collectives  20.5 us (2%)
  between operations  16.1 us (1%)
    psum x1, waiting for transfers between devices, per_device(): lax.psum(jnp.dot(activated_low, fc2_weight, preferred_element_type=jnp.fl...  427 us
    psum x1, waiting for transfers between devices, per_device(): lax.psum(jnp.dot(attended_low, proj_weight, preferred_element_type=jnp.fl...  218 us
    psum x1, waiting for transfers between devices, per_device(): lax.psum(jnp.einsum('rf,df->rd', grad_hidden_low, fc1_weight, preferred_e...  218 us
    unnamed x147, local copies, waits for them, and re-layouts  37.7 us
    reduce_scatter x1, waiting for transfers between devices, per_device(): lax.psum_scatter(grad_qkv_weight, 'inner', scatter_dimension=0, tiled=True)  36.2 us
    reduce_scatter x1, waiting for transfers between devices, per_device(): lax.psum_scatter(grad_fc2_weight, 'inner', scatter_dimension=1, tiled=True)  35.8 us
    reduce_scatter x1, waiting for transfers between devices, per_device(): lax.psum_scatter(grad_fc1_weight, 'inner', scatter_dimension=0, tiled=True)  28.4 us
  transfers between devices with their start and end apart: 10, of which 8 were waited for; matrix products, arithmetic and copies ran while one was open for 9% of the time, Pallas kernels for 0%

commit v1 on v0

v1 whole, which is shorter than its diff:
```python
import functools

import jax
import jax.numpy as jnp
from jax import lax
from jax.experimental import pallas as pl
from jax.experimental.pallas import tpu as pltpu
from jax.sharding import PartitionSpec as P

HEAD_DIM = 64
EPS = 1e-06
F32 = jnp.float32
BF16 = jnp.bfloat16
NEG = -1e30
LANES = 128
WIDE = 256
MAIN = 256
VMEM_LIMIT = 56 * 1024 * 1024
PLANE = ("inner", "outer")


def mm_nt(a, b):
    return lax.dot_general(a, b, (((1,), (1,)), ((), ())), preferred_element_type=F32)


def mm_nn(a, b):
    return lax.dot_general(a, b, (((1,), (0,)), ((), ())), preferred_element_type=F32)


def mm_tn(a, b):
    return lax.dot_general(a, b, (((0,), (0,)), ((), ())), preferred_element_type=F32)


def params():
    return pltpu.CompilerParams(vmem_limit_bytes=VMEM_LIMIT)


def block(shape):
    return pl.BlockSpec((1,) + tuple(shape[1:]), lambda c: (c,) + (0,) * (len(shape) - 1))


def whole(shape):
    return pl.BlockSpec(tuple(shape), lambda c: (0,) * len(shape))


def row_sum(x):
    return jnp.sum(x, 0, keepdims=True)


def norm_parts(v):
    center = v - jnp.mean(v, -1, keepdims=True)
    rstd = lax.rsqrt(jnp.mean(center * center, -1, keepdims=True) + EPS)
    return center * rstd, rstd


def norm_back(xhat, rstd, u, gain):
    gu = u * gain
    return (
        gu - jnp.mean(gu, -1, keepdims=True) - xhat * jnp.mean(gu * xhat, -1, keepdims=True)
    ) * rstd


def put_columns(ref, rows, x):
    for j in range(ref.shape[0]):
        ref[j, rows, :] = x[:, j * LANES : (j + 1) * LANES]


def get_columns(ref, rows):
    return jnp.concatenate([ref[j, rows, :] for j in range(ref.shape[0])], 1)


def enter_kernel(tok_ref, cot_ref, flag_ref, vec_ref, pos_ref, begin_ref, n1_ref, up_ref, tok_s, cot_s):
    seq, crops, _ = tok_ref.shape
    rows = pos_ref.shape[0]
    step = 29 if seq % 29 == 0 else 1

    @pl.when(pl.program_id(0) == 0)
    def _():
        def move(i, carry):
            part = pl.ds(i * step, step)
            dst = pl.ds(pl.multiple_of(i * (step * crops), crops), step * crops)
            for src, out in ((tok_ref, tok_s), (cot_ref, cot_s)):
                put_columns(out, dst, src[part].astype(F32).reshape(step * crops, -1))
            return carry

        lax.fori_loop(0, seq // step, move, 0)
        for out in (tok_s, cot_s):
            out[:, seq * crops :, :] = jnp.zeros_like(out[:, seq * crops :, :])

    mine = pl.ds(pl.program_id(0), rows, stride=crops)
    flagged = flag_ref[0][:, 0:1] > 0.5
    begin = jnp.where(flagged, vec_ref[0:1, :], get_columns(tok_s, mine)) + pos_ref[...]
    begin_ref[0] = begin
    xhat, _ = norm_parts(begin)
    n1_ref[0] = (xhat * vec_ref[1:2, :] + vec_ref[2:3, :]).astype(BF16)
    up_ref[0] = get_columns(cot_s, mine).astype(BF16)


def enter(tok, cot, flags, vecs, pos):
    seq, crops, width = tok.shape
    rows = pos.shape[0]
    shape = (crops, rows, width)
    return pl.pallas_call(
        enter_kernel,
        grid=(crops,),
        in_specs=[whole(tok.shape), whole(cot.shape), block(flags.shape), whole(vecs.shape), whole(pos.shape)],
        out_specs=[block(shape)] * 3,
        out_shape=[
            jax.ShapeDtypeStruct(shape, F32),
            jax.ShapeDtypeStruct(shape, BF16),
            jax.ShapeDtypeStruct(shape, BF16),
        ],
        scratch_shapes=[pltpu.VMEM((width // LANES, rows * crops, LANES), F32)] * 2,
        compiler_params=params(),
        name="enter",
    )(tok, cot, flags, vecs, pos)


def head_masks(heads):
    lane = lax.broadcasted_iota(jnp.int32, (1, WIDE), 1)
    return [((lane // HEAD_DIM) == h).astype(F32) for h in range(heads)], lane


def per_head_rows(x, masks):
    parts = [x * m for m in masks]
    parts.append(jnp.zeros((LANES - 8 * len(masks), x.shape[1]), F32))
    return jnp.concatenate(parts, 0).astype(BF16)


def pick(index, parts):
    out = parts[-1]
    for h in range(len(parts) - 2, -1, -1):
        out = jnp.where(index == h, parts[h], out)
    return out


def attention_forward(n1, w_ref, bias, heads, tail_valid):
    masks, lane = head_masks(heads)
    low = [m.astype(BF16) for m in masks]
    head_width = heads * HEAD_DIM
    mixed = (mm_nt(n1, w_ref[0 : 3 * WIDE, :]) + bias).astype(BF16)
    q = mixed[:, 0:WIDE] * jnp.asarray(HEAD_DIM**-0.5, BF16)
    k, v = mixed[:, WIDE : 2 * WIDE], mixed[:, 2 * WIDE : 3 * WIDE]
    mixed = jnp.concatenate([q, k, v], 1)
    k_main, v_main = k[0:MAIN], v[0:MAIN]
    v_masks = [m + (lane == head_width + h).astype(F32) for h, m in enumerate(masks)]
    k_tail = per_head_rows(k[MAIN : MAIN + 8].astype(F32), masks)
    v_tail = per_head_rows(v[MAIN : MAIN + 8].astype(F32), v_masks)
    col = lax.broadcasted_iota(jnp.int32, (1, LANES), 1)
    valid = (col < 8 * heads) & ((col % 8) < tail_valid)
    s_tail = jnp.where(valid, mm_nt(q, k_tail), NEG)
    tops, total = [], None
    for h in range(heads):
        s = mm_nt(q * low[h], k_main)
        top = jnp.where((col // 8) == h, s_tail, NEG)
        for i in range(MAIN // LANES):
            top = jnp.maximum(top, s[:, i * LANES : (i + 1) * LANES])
        top = jnp.max(top, -1, keepdims=True)
        tops.append(top)
        part = mm_nn(jnp.exp(s - top).astype(BF16), v_main * v_masks[h].astype(BF16))
        total = part if total is None else total + part
    e_tail = jnp.exp(s_tail - pick(col // 8, tops)).astype(BF16)
    total = total + mm_nn(e_tail, v_tail)
    sums = [total[:, head_width + h : head_width + h + 1] for h in range(heads)]
    scale = pick(lane // HEAD_DIM, [1.0 / s for s in sums])
    attended = (total * scale).astype(BF16)
    log_total = pick(col, [t + jnp.log(s) for t, s in zip(tops, sums)])
    branch = mm_nn(attended, w_ref[3 * WIDE : 4 * WIDE, :])
    return mixed, log_total, attended, branch


def place_pieces(info_ref, pieces, out_ref, base, first):
    p, core = info_ref[0], info_ref[1]
    own, along, far, peer_a, peer_b = pieces
    q = p ^ 2
    a_bit = jnp.where(core == 0, 4, 1)
    b_bit = 5 - a_bit
    spots = (
        (own, None, p),
        (along, None, p ^ a_bit),
        (far, 0, p ^ b_bit),
        (far, 1, p ^ 5),
        (peer_a, 0, q),
        (peer_a, 1, q ^ b_bit),
        (peer_b, 0, q ^ a_bit),
        (peer_b, 1, q ^ 5),
    )
    size = out_ref.shape[0]
    for ref, slot, ident in spots:
        view = ref if slot is None else ref.at[slot]
        rows = 96
        dst = pl.multiple_of(first(ident), 32)
        out_ref[pl.ds(dst, rows), :] = view[base : base + rows, :].astype(BF16)


def attn_kernel(*refs, heads, tail_valid, gathered, accs, finish):
    it = iter(refs)
    if gathered:
        info = next(it)
    n1_ref, bias_ref = next(it), next(it)
    if gathered:
        pieces = [next(it) for _ in range(5)]
    else:
        w_ref = next(it)
    acc_refs = [next(it) for _ in range(accs)]
    if finish:
        begin_ref, vec_ref = next(it), next(it)
    br_ref, mix_ref, lse_ref = next(it), next(it), next(it)
    if gathered:
        w_ref = next(it)

        @pl.when(pl.program_id(0) == 0)
        def _():
            for i in range(4):
                w_ref[i * WIDE + 192 : (i + 1) * WIDE, :] = jnp.zeros((WIDE - 192, w_ref.shape[1]), BF16)
            place_pieces(info, pieces, w_ref, 0, lambda i: (i >> 1) * WIDE + (i & 1) * 96)

    if not gathered:
        att_ref = next(it)
    mixed, log_total, attended, branch = attention_forward(
        n1_ref[0], w_ref, bias_ref[...], heads, tail_valid
    )
    mix_ref[0] = mixed
    lse_ref[0] = log_total
    if not gathered:
        att_ref[0] = attended
    for ref in acc_refs:
        branch = branch + ref[0]
    br_ref[0] = branch
    if finish:
        n2_ref = next(it)
        middle = begin_ref[0] + vec_ref[0:1, :] * (branch + vec_ref[1:2, :])
        xhat, _ = norm_parts(middle)
        n2_ref[0] = (xhat * vec_ref[2:3, :] + vec_ref[3:4, :]).astype(BF16)


def attn(n1, bias, weights, info, accs, heads, tail_valid, finish=None):
    crops, rows, width = n1.shape
    gathered = info is not None
    args, specs = [], []

    def add(x, spec):
        args.append(x)
        specs.append(spec)

    if gathered:
        add(info, pl.BlockSpec(memory_space=pltpu.SMEM))
    add(n1, block(n1.shape))
    add(bias, whole(bias.shape))
    for w in weights:
        add(w, whole(w.shape))
    for a in accs:
        add(a, block(a.shape))
    if finish is not None:
        add(finish[0], block(finish[0].shape))
        add(finish[1], whole(finish[1].shape))
    outs = [
        ((crops, rows, width), F32, block),
        ((crops, rows, 3 * WIDE), BF16, block),
        ((crops, rows, LANES), F32, block),
    ]
    if gathered:
        outs.append(((4 * WIDE, width), BF16, whole))
    else:
        outs.append(((crops, rows, WIDE), BF16, block))
    if finish is not None:
        outs.append(((crops, rows, width), BF16, block))
    return pl.pallas_call(
        functools.partial(
            attn_kernel,
            heads=heads,
            tail_valid=tail_valid,
            gathered=gathered,
            accs=len(accs),
            finish=finish is not None,
        ),
        grid=(crops,),
        in_specs=specs,
        out_specs=[kind(shape) for shape, _, kind in outs],
        out_shape=[jax.ShapeDtypeStruct(shape, dtype) for shape, dtype, _ in outs],
        compiler_params=params(),
        name="attention",
    )(*args)


def attention_backward(gb, w_ref, mix_ref, lse_ref, heads, tail_valid):
    masks, lane = head_masks(heads)
    low = [m.astype(BF16) for m in masks]
    da = mm_nt(gb, w_ref[3 * WIDE : 4 * WIDE, :]).astype(BF16)
    q, k, v = (mix_ref[0, :, i * WIDE : (i + 1) * WIDE] for i in range(3))
    k_main, v_main = k[0:MAIN], v[0:MAIN]
    k_tail = per_head_rows(k[MAIN : MAIN + 8].astype(F32), masks)
    v_tail = per_head_rows(v[MAIN : MAIN + 8].astype(F32), masks)
    col = lax.broadcasted_iota(jnp.int32, (1, LANES), 1)
    valid = (col < 8 * heads) & ((col % 8) < tail_valid)
    lse = [lse_ref[0, :, h : h + 1] for h in range(heads)]
    p_tail = jnp.where(valid, jnp.exp(mm_nt(q, k_tail) - pick(col // 8, lse)), 0.0)
    dp_tail = mm_nt(da, v_tail)
    x_tail = p_tail * dp_tail
    dq = dk = dv = None
    deltas = []
    for h in range(heads):
        qh, dah = q * low[h], da * low[h]
        p = jnp.exp(mm_nt(qh, k_main) - lse[h])
        dp = mm_nt(dah, v_main)
        x = p * dp
        delta = jnp.where((col // 8) == h, x_tail, 0.0)
        for i in range(MAIN // LANES):
            delta = delta + x[:, i * LANES : (i + 1) * LANES]
        delta = jnp.sum(delta, -1, keepdims=True)
        deltas.append(delta)
        ds = (p * (dp - delta)).astype(BF16)
        one = mm_nn(ds, k_main * low[h])
        two = mm_tn(ds, qh)
        three = mm_tn(p.astype(BF16), dah)
        dq = one if dq is None else dq + one
        dk = two if dk is None else dk + two
        dv = three if dv is None else dv + three
    ds_tail = (p_tail * (dp_tail - pick(col // 8, deltas))).astype(BF16)
    dq = (dq + mm_nn(ds_tail, k_tail)) * (HEAD_DIM**-0.5)
    dk_tail = mm_tn(ds_tail, q)
    dv_tail = mm_tn(p_tail.astype(BF16), da)
    dk_tail = sum(dk_tail[8 * h : 8 * h + 8] * masks[h] for h in range(heads))
    dv_tail = sum(dv_tail[8 * h : 8 * h + 8] * masks[h] for h in range(heads))
    rest = jnp.zeros((gb.shape[0] - MAIN - 8, WIDE), F32)
    dk = jnp.concatenate([dk, dk_tail, rest], 0)
    dv = jnp.concatenate([dv, dv_tail, rest], 0)
    return dq, dk, dv


def attn_back_kernel(*refs, heads, tail_valid, own, accs, finish):
    it = iter(refs)
    gb_ref, w_ref, mix_ref, lse_ref = (next(it) for _ in range(4))
    acc_refs = [next(it) for _ in range(accs)]
    if finish:
        begin_ref, gmid_ref, flag_ref, vec_ref = (next(it) for _ in range(4))
    else:
        gn_ref = next(it)
    first = pl.program_id(0) == 0
    dq, dk, dv = attention_backward(gb_ref[0], w_ref, mix_ref, lse_ref, heads, tail_valid)
    gm = jnp.concatenate([dq, dk, dv], 1).astype(BF16)
    if own:
        gm_ref, sum_ref = next(it), next(it)
        gm_ref[0] = gm
        sums = jnp.concatenate([row_sum(dq), row_sum(dv), jnp.zeros((6, WIDE), F32)], 0)
        sum_ref[...] = jnp.where(first, sums, sum_ref[...] + sums)
    gn = mm_nn(gm, w_ref[0 : 3 * WIDE, :])
    for ref in acc_refs:
        gn = gn + ref[0]
    if not finish:
        gn_ref[0] = gn
        return
    gtok_ref, gpos_ref, sum_ref, gtok_s = (next(it) for _ in range(4))
    xhat, rstd = norm_parts(begin_ref[0])
    grad_begin = gmid_ref[0] + norm_back(xhat, rstd, gn, vec_ref[0:1, :])
    flagged = flag_ref[0][:, 0:1] > 0.5
    cleared = jnp.where(flagged, 0.0, grad_begin)
    seq = gtok_ref.shape[0] // 8
    put_columns(gtok_s, pl.ds(pl.program_id(0), cleared.shape[0], stride=8), cleared)
    sums = jnp.concatenate(
        [
            row_sum(gn * xhat),
            row_sum(gn),
            row_sum(grad_begin - cleared),
            jnp.zeros((5, gn.shape[1]), F32),
        ],
        0,
    )

    @pl.when(first)
    def _():
        sum_ref[...] = sums
        gpos_ref[...] = grad_begin

    @pl.when(jnp.logical_not(first))
    def _():
        sum_ref[...] += sums
        gpos_ref[...] += grad_begin

    @pl.when(pl.program_id(0) == pl.num_programs(0) - 1)
    def _():
        for j in range(gtok_s.shape[0]):
            gtok_ref[:, j * LANES : (j + 1) * LANES] = gtok_s[j, 0 : seq * 8, :]


def attn_back(gb, w, mixed, lse, accs, heads, tail_valid, own=False, finish=None, seq=None):
    crops, rows, width = gb.shape
    args = [gb, w, mixed, lse, *accs]
    specs = [block(gb.shape), whole(w.shape), block(mixed.shape), block(lse.shape)]
    specs += [block(a.shape) for a in accs]
    outs, scratch = [], []
    if finish is not None:
        begin, gmid, flags, vecs = finish
        args += [begin, gmid, flags, vecs]
        specs += [block(begin.shape), block(gmid.shape), block(flags.shape), whole(vecs.shape)]
        scratch.append(pltpu.VMEM((width // LANES, rows * crops, LANES), F32))
    else:
        outs.append(((crops, rows, width), F32, block))
    if own:
        outs += [((crops, rows, 3 * WIDE), BF16, block), ((8, WIDE), F32, whole)]
    if finish is not None:
        outs += [
            ((seq * crops, width), F32, whole),
            ((rows, width), F32, whole),
            ((8, width), F32, whole),
        ]
    return pl.pallas_call(
        functools.partial(
            attn_back_kernel,
            heads=heads,
            tail_valid=tail_valid,
            own=own,
            accs=len(accs),
            finish=finish is not None,
        ),
        grid=(crops,),
        in_specs=specs,
        out_specs=[kind(shape) for shape, _, kind in outs],
        out_shape=[jax.ShapeDtypeStruct(shape, dtype) for shape, dtype, _ in outs],
        scratch_shapes=scratch,
        compiler_params=params(),
        name="attention_back",
    )(*args)


def gelu_and_slope(h):
    phi = 0.5 * (1.0 + lax.erf(h * (2.0**-0.5)))
    bell = jnp.exp(-0.5 * h * h) * 0.3989422804014327
    return h * phi, phi + h * bell


def mlp_kernel(*refs, gathered, accs, own, finish):
    it = iter(refs)
    if gathered:
        info = next(it)
    n2_ref, up_ref, vec_ref, bias_ref = (next(it) for _ in range(4))
    if gathered:
        pieces = [next(it) for _ in range(5)]
    else:
        w1_ref, w2_ref = next(it), next(it)
    acc_refs = [(next(it), next(it)) for _ in range(accs)]
    if finish:
        begin_ref, br_ref = next(it), next(it)
        res_ref, gmid_ref, gb_ref, sum_ref = (next(it) for _ in range(4))
    else:
        out_ref, gn_ref = next(it), next(it)
    if own:
        a_ref, gh_ref, go_ref, hsum_ref = (next(it) for _ in range(4))
    first = pl.program_id(0) == 0
    if finish:
        res_s = next(it)
    if gathered:
        w1_ref, w2_ref = next(it), next(it)

        @pl.when(first)
        def _():
            place_pieces(info, pieces, w1_ref, 0, lambda i: i * 96)
            place_pieces(info, pieces, w2_ref, 96, lambda i: i * 96)

    up = up_ref[0].astype(F32)
    grad_output = up * vec_ref[0:1, :]
    go = grad_output.astype(BF16)
    n2 = n2_ref[0]
    a, slope = gelu_and_slope(mm_nt(n2, w1_ref[...]) + bias_ref[...])
    a = a.astype(BF16)
    gh = mm_nt(go, w2_ref[...]) * slope
    if own:
        a_ref[0] = a
        go_ref[0] = go
        sums = jnp.concatenate([row_sum(gh), jnp.zeros((7, gh.shape[1]), F32)], 0)
        hsum_ref[...] = jnp.where(first, sums, hsum_ref[...] + sums)
    gh = gh.astype(BF16)
    if own:
        gh_ref[0] = gh
    out = mm_nn(a, w2_ref[...])
    gn = mm_nn(gh, w1_ref[...])
    for o_ref, g_ref in acc_refs:
        out = out + o_ref[0]
        gn = gn + g_ref[0]
    if not finish:
        out_ref[0] = out
        gn_ref[0] = gn
        return
    mlp_scale, fc2_bias, attn_scale, proj_bias, gain = (vec_ref[i : i + 1, :] for i in range(5))
    out = out + fc2_bias
    branch = br_ref[0] + proj_bias
    middle = begin_ref[0] + attn_scale * branch
    result = middle + mlp_scale * out
    rows = result.shape[0]
    crops = 8
    put_columns(res_s, pl.ds(pl.program_id(0), rows, stride=crops), result)
    xhat, rstd = norm_parts(middle)
    gmid = up + norm_back(xhat, rstd, gn, gain)
    gmid_ref[0] = gmid
    gbr = gmid * attn_scale
    gb_ref[0] = gbr.astype(BF16)
    sums = jnp.concatenate(
        [
            row_sum(up * out),
            row_sum(grad_output),
            row_sum(gn * xhat),
            row_sum(gn),
            row_sum(gmid * branch),
            row_sum(gbr),
            jnp.zeros((2, gn.shape[1]), F32),
        ],
        0,
    )
    sum_ref[...] = jnp.where(first, sums, sum_ref[...] + sums)

    @pl.when(pl.program_id(0) == pl.num_programs(0) - 1)
    def _():
        seq = res_ref.shape[0]
        step = 29 if seq % 29 == 0 else 1

        def move(i, carry):
            src = pl.ds(pl.multiple_of(i * (step * crops), crops), step * crops)
            res_ref[pl.ds(i * step, step)] = get_columns(res_s, src).reshape(step, crops, -1).astype(BF16)
            return carry

        lax.fori_loop(0, seq // step, move, 0)


def mlp(n2, up, vecs, bias, weights, info, accs, own=False, finish=None, seq=None):
    crops, rows, width = n2.shape
    hidden = bias.shape[1]
    gathered = info is not None
    args, specs = [], []

    def add(x, spec):
        args.append(x)
        specs.append(spec)

    if gathered:
        add(info, pl.BlockSpec(memory_space=pltpu.SMEM))
    add(n2, block(n2.shape))
    add(up, block(up.shape))
    add(vecs, whole(vecs.shape))
    add(bias, whole(bias.shape))
    for w in weights:
        add(w, whole(w.shape))
    for pair in accs:
        for a in pair:
            add(a, block(a.shape))
    full = (crops, rows, width)
    scratch = []
    if finish is not None:
        add(finish[0], block(finish[0].shape))
        add(finish[1], block(finish[1].shape))
        outs = [
            ((seq, crops, width), BF16, whole),
            (full, F32, block),
            (full, BF16, block),
            ((8, width), F32, whole),
        ]
        scratch.append(pltpu.VMEM((width // LANES, rows * crops, LANES), F32))
    else:
        outs = [(full, F32, block), (full, F32, block)]
    if own:
        outs += [((crops, rows, hidden), BF16, block)] * 2 + [(full, BF16, block), ((8, hidden), F32, whole)]
    if gathered:
        scratch += [pltpu.VMEM((hidden, width), BF16)] * 2
    return pl.pallas_call(
        functools.partial(mlp_kernel, gathered=gathered, accs=len(accs), own=own, finish=finish is not None),
        grid=(crops,),
        in_specs=specs,
        out_specs=[kind(shape) for shape, _, kind in outs],
        out_shape=[jax.ShapeDtypeStruct(shape, dtype) for shape, dtype, _ in outs],
        scratch_shapes=scratch,
        compiler_params=params(),
        name="mlp",
    )(*args)


def weight_grad_kernel(x1_ref, y1_ref, x2_ref, y2_ref, o1_ref, o2_ref):
    o1_ref[...] = mm_tn(x1_ref[...], y1_ref[...])
    o2_ref[...] = mm_tn(x2_ref[...], y2_ref[...])


def weight_grads(x1, y1, x2, y2):
    rows, width = x1.shape
    col = pl.BlockSpec((rows, WIDE), lambda i: (0, i))

    def out(y):
        return pl.BlockSpec((WIDE, y.shape[1]), lambda i: (i, 0))

    return pl.pallas_call(
        weight_grad_kernel,
        grid=(width // WIDE,),
        in_specs=[col, whole(y1.shape), col, whole(y2.shape)],
        out_specs=[out(y1), out(y2)],
        out_shape=[jax.ShapeDtypeStruct((width, y.shape[1]), F32) for y in (y1, y2)],
        compiler_params=params(),
        name="weight_grads",
    )(x1, y1, x2, y2)


def plane_perm(inner, outer, move):
    pairs = []
    for i in range(inner):
        for o in range(outer):
            j, r = move(i, o)
            pairs.append((i * outer + o, j * outer + r))
    return pairs


def spread(piece, perms):
    one, two, three = perms
    along = lax.ppermute(piece, PLANE, one)
    both = jnp.stack([piece, along])
    far = lax.ppermute(both, PLANE, two)
    peer_a = lax.ppermute(both, PLANE, three)
    peer_b = lax.ppermute(far, PLANE, three)
    return [piece, along, far, peer_a, peer_b]


def reduce_inner(x):
    return lax.psum(lax.psum_scatter(x, "inner", scatter_dimension=0, tiled=True), "outer")


def per_device(
    sizes,
    tokens,
    patch_mask,
    cotangent,
    mask_token,
    pos_embed,
    pre_attn_gain,
    pre_attn_bias,
    qkv_weight,
    qv_bias,
    proj_weight,
    proj_bias,
    attn_scale,
    pre_mlp_gain,
    pre_mlp_bias,
    fc1_weight,
    fc1_bias,
    fc2_weight,
    fc2_bias,
    mlp_scale,
):
    tensor_n, inner_n, outer_n = sizes
    crops, seq, width = tokens.shape
    head_width = qkv_weight.shape[2]
    heads = head_width // HEAD_DIM
    hidden = fc1_weight.shape[1]
    rows = -(-seq // 16) * 16
    tail_valid = seq - MAIN
    t = lax.axis_index("tensor")
    inner = lax.axis_index("inner")
    outer = lax.axis_index("outer")
    place = inner * 2 + outer % 2
    info = jnp.stack([place, inner % 2]).astype(jnp.int32)

    qkv_rows = qkv_weight.transpose(1, 2, 0).reshape(3 * head_width, width)
    own_attn = jnp.concatenate([qkv_rows, proj_weight], 0)
    own_fc1 = fc1_weight.T
    part = width // 8

    def eighth(x):
        return lax.dynamic_slice_in_dim(x, place * part, part, 0).astype(F32)

    attn_piece = eighth(own_attn)
    mlp_piece = jnp.concatenate([eighth(own_fc1), eighth(fc2_weight)], 0)
    perms = (
        plane_perm(inner_n, outer_n, lambda i, o: (i, o ^ 1) if i % 2 else (i ^ 2, o)),
        plane_perm(inner_n, outer_n, lambda i, o: (i ^ 2, o) if i % 2 else (i, o ^ 1)),
        plane_perm(inner_n, outer_n, lambda i, o: (i ^ 1, o)),
    )
    hops = [[(i, i ^ k) for i in range(tensor_n)] for k in range(1, tensor_n)]
    attn_parts = [spread(lax.ppermute(attn_piece, "tensor", hop), perms) for hop in hops]
    mlp_parts = [spread(lax.ppermute(mlp_piece, "tensor", hop), perms) for hop in hops]
    all_biases = lax.all_gather(jnp.concatenate([qv_bias.reshape(-1), fc1_bias]), "tensor")

    def biases_of(k):
        one = lax.dynamic_index_in_dim(all_biases, t ^ k, 0, keepdims=False)
        q_bias, v_bias = one[0:head_width], one[head_width : 2 * head_width]
        ones = jnp.ones((heads,), F32)
        gap = jnp.zeros((WIDE - head_width - heads,), F32)
        zeros = jnp.zeros((WIDE,), F32)
        row = jnp.concatenate([q_bias, zeros[head_width:], zeros, v_bias, ones, gap])
        return row[None, :], one[2 * head_width :][None, :]

    biases = [biases_of(k) for k in range(tensor_n)]

    flag = jnp.concatenate(
        [
            jnp.zeros((crops, seq - patch_mask.shape[1]), F32),
            (patch_mask == 1).astype(F32),
            jnp.zeros((crops, rows - seq), F32),
        ],
        1,
    )
    flags = jnp.broadcast_to(flag[:, :, None], (crops, rows, LANES))
    pos = jnp.pad(pos_embed, ((0, rows - seq), (0, 0)))
    begin, n1, up = enter(
        tokens.transpose(1, 0, 2),
        cotangent.transpose(1, 0, 2),
        flags,
        jnp.stack([mask_token, pre_attn_gain, pre_attn_bias]),
        pos,
    )

    gap_rows = jnp.zeros((WIDE - head_width, width), BF16)
    own_w = jnp.concatenate(
        sum(
            ([own_attn[i * head_width : (i + 1) * head_width], gap_rows] for i in range(4)),
            [],
        ),
        0,
    )
    attn_vecs = jnp.stack([attn_scale, proj_bias, pre_mlp_gain, pre_mlp_bias])
    run = functools.partial(attn, heads=heads, tail_valid=tail_valid)
    br0, mix0, lse0, att0 = run(n1, biases[0][0], [own_w], None, [])
    br1, mix1, lse1, w_1 = run(n1, biases[1][0], attn_parts[0], info, [br0])
    br2, mix2, lse2, w_2 = run(n1, biases[2][0], attn_parts[1], info, [])
    br, mix3, lse3, w_3, n2 = run(
        n1, biases[3][0], attn_parts[2], info, [br2, br1], finish=(begin, attn_vecs)
    )

    mlp_vecs = jnp.stack([mlp_scale, fc2_bias, attn_scale, proj_bias, pre_mlp_gain])
    out0, gn0, a0, gh0, go0, hsum = mlp(
        n2, up, mlp_vecs, biases[0][1], [own_fc1, fc2_weight], None, [], own=True
    )
    flat = lambda x: x.reshape(crops * rows, -1)
    grad_fc1, grad_fc2 = weight_grads(flat(n2), flat(gh0), flat(go0), flat(a0))
    shares_mlp = reduce_inner(jnp.concatenate([grad_fc1, grad_fc2], 1))
    acc1 = mlp(n2, up, mlp_vecs, biases[1][1], mlp_parts[0], info, [(out0, gn0)])
    acc2 = mlp(n2, up, mlp_vecs, biases[2][1], mlp_parts[1], info, [])
    result, gmid, gb, mid_sums = mlp(
        n2, up, mlp_vecs, biases[3][1], mlp_parts[2], info, [acc2, acc1], finish=(begin, br), seq=seq
    )

    back = functools.partial(attn_back, heads=heads, tail_valid=tail_valid)
    gn0, gm0, qv_sums = back(gb, own_w, mix0, lse0, [], own=True)
    grad_qkv, grad_proj = weight_grads(flat(n1), flat(gm0), flat(gb), flat(att0))
    pieces = [grad_qkv[:, i * WIDE : i * WIDE + head_width] for i in range(3)]
    shares_attn = reduce_inner(jnp.concatenate(pieces + [grad_proj[:, :head_width]], 1))
    (gn1,) = back(gb, w_1, mix1, lse1, [gn0])
    (gn2,) = back(gb, w_2, mix2, lse2, [])
    gtok, gpos, last_sums = back(
        gb, w_3, mix3, lse3, [gn2, gn1], finish=(begin, gmid, flags, pre_attn_gain[None, :]), seq=seq
    )

    quarter = width // inner_n
    small = head_width // inner_n

    def spaced(x):
        return jnp.pad(x.reshape(inner_n, small), ((0, 0), (0, quarter - small))).reshape(1, width)

    pack = jnp.concatenate(
        [
            gpos[:seq],
            mid_sums[0:6],
            last_sums[0:3],
            hsum[0:1],
            spaced(qv_sums[0, :head_width]),
            spaced(qv_sums[1, :head_width]),
        ],
        0,
    )
    pack = pack.reshape(-1, inner_n, quarter).transpose(1, 0, 2).reshape(-1, quarter)
    small_sums = reduce_inner(pack)
    vec = lambda i: small_sums[seq + i]
    grad_qkv = shares_attn[:, : 3 * head_width].reshape(-1, 3, head_width)
    return (
        result.transpose(1, 0, 2),
        gtok.reshape(seq, crops, width).transpose(1, 0, 2),
        vec(8),
        small_sums[:seq],
        vec(6),
        vec(7),
        grad_qkv,
        jnp.stack([vec(10)[:small], vec(11)[:small]]),
        shares_attn[:, 3 * head_width :].T,
        vec(5),
        vec(4),
        vec(2),
        vec(3),
        shares_mlp[:, :hidden],
        vec(9),
        shares_mlp[:, hidden:].T,
        vec(1),
        vec(0),
    )


def solution(mesh):
    in_specs = (
        P(("inner", "outer"), None, None),
        P(("inner", "outer"), None),
        P(("inner", "outer"), None, None),
        P(),
        P(),
        P(),
        P(),
        P(None, None, "tensor"),
        P(None, "tensor"),
        P("tensor", None),
        P(),
        P(),
        P(),
        P(),
        P(None, "tensor"),
        P("tensor"),
        P("tensor", None),
        P(),
        P(),
    )
    out_specs = (
        P(("inner", "outer"), None, None),
        P(("inner", "outer"), None, None),
        P("inner"),
        P(None, "inner"),
        P("inner"),
        P("inner"),
        P("inner", None, "tensor"),
        P(None, ("tensor", "inner")),
        P("tensor", "inner"),
        P("inner"),
        P("inner"),
        P("inner"),
        P("inner"),
        P("inner", "tensor"),
        P(("tensor", "inner")),
        P("tensor", "inner"),
        P("inner"),
        P("inner"),
    )
    sizes = tuple(mesh.shape[name] for name in ("tensor", "inner", "outer"))
    return jax.shard_map(
        functools.partial(per_device, sizes),
        mesh=mesh,
        in_specs=in_specs,
        out_specs=out_specs,
        check_vma=False,
    )
```

time: 1350 us -> 632 us (0.47)
  waiting for transfers between devices: 1010 us -> 219 us
  Pallas kernels: 0 us -> 278 us
  matrix products: 110 us -> 0 us
  other arithmetic: 99.8 us -> 19.5 us
  local copies, waits for them, and re-layouts: 86.2 us -> 44.1 us
  starting transfers between devices: 0.81 us -> 28.2 us
    psum x4 -> x1, waiting for transfers between devices: 886 us -> 65.5 us  [reduce_inner(): lax.psum(lax.psum_scatter(x, 'inner', scatter_dimension=0, tiled=True), '...]
    pallas_call x0 -> x15, Pallas kernels: none -> 278 us  [the longest x4 96.9 us: attn_back(): pl.pallas_call(functools.partial(attn_back_kernel, heads=heads, tail_vali...]
    dot_general x16 -> x0, matrix products: 102 us -> none  [the longest x1 18.6 us: per_device(): jnp.dot(normed_mlp_low, fc1_weight, preferred_element_type=jnp.float32)]
    reduce_sum x16 -> x0, other arithmetic: 82.5 us -> none  [the longest x4 26.3 us: layer_norm(): center = field - jnp.mean(field, -1, keepdims=True)]
    ppermute x0 -> x30, waiting for transfers between devices: none -> 65.9 us  [the longest x3 24 us: per_device(): lax.ppermute(mlp_piece, 'tensor', hop)]
    reshape x7 -> x2, local copies, waits for them, and re-layouts: 33.1 us -> 1.57 us  [the longest x1 1.49 us: per_device(): pack.reshape(-1, inner_n, quarter).transpose(1, 0, 2).reshape(-1, quarter)]
    ppermute x0 -> x30, starting transfers between devices: none -> 28 us  [the longest x6 7.27 us: spread(): along = lax.ppermute(piece, PLANE, one)]
    unnamed x147 -> x99, local copies, waits for them, and re-layouts: 37.7 us -> 10.1 us
  transfers between devices with their start and end apart: 10 -> 34, of which waited for: 8 -> 13; matrix products, arithmetic and copies ran while one was open for 9% -> 6% of each run, Pallas kernels for 0% -> 24%
where the time goes in v1:
time: 632 us; the launch traced here: 627 us
  Pallas kernels  278 us (44%)
  waiting for transfers between devices  219 us (35%)
  local copies, waits for them, and re-layouts  44.1 us (7%)
  starting transfers between devices  28.2 us (4%)
  blocking collectives  23.1 us (4%)
  other arithmetic  19.5 us (3%)
  between operations  15.6 us (2%)
    pallas_call x4, Pallas kernels, attn_back(): pl.pallas_call(functools.partial(attn_back_kernel, heads=heads, tail_vali...  96.9 us
    reduce_scatter x2, waiting for transfers between devices, reduce_inner(): lax.psum_scatter(x, 'inner', scatter_dimension=0, tiled=True)  84.6 us
    pallas_call x4, Pallas kernels, mlp(): pl.pallas_call(functools.partial(mlp_kernel, gathered=gathered, accs=len(...  80 us
    pallas_call x4, Pallas kernels, attn(): pl.pallas_call(functools.partial(attn_kernel, heads=heads, tail_valid=tai...  69.3 us
    psum x1, waiting for transfers between devices, reduce_inner(): lax.psum(lax.psum_scatter(x, 'inner', scatter_dimension=0, tiled=True), '...  65.5 us
    ppermute x3, waiting for transfers between devices, per_device(): lax.ppermute(mlp_piece, 'tensor', hop)  24 us
    all_gather x1, blocking collectives, per_device(): lax.all_gather(jnp.concatenate([qv_bias.reshape(-1), fc1_bias]), 'tensor')  23.1 us
    pallas_call x2, Pallas kernels, weight_grads(): pl.pallas_call(weight_grad_kernel, grid=(width // WIDE,), in_specs=[col,...  19.6 us
  transfers between devices with their start and end apart: 34, of which 13 were waited for; matrix products, arithmetic and copies ran while one was open for 6% of the time, Pallas kernels for 24%

profile of v1, /device:TPU:0, one launch (start us, length us, event | category | flops | bytes accessed | tf_op | source)
XLA Modules:
  0.0 627.0 jit_solution(13329976987248872111)
XLA Ops:
  7.3 1.8 fusion.4
  9.0 3.0 collective-permute-start.10
  12.1 2.6 collective-permute-start.5
  16.5 8.3 %collective-permute-done.10.refs_3_ = f32[96,768]{1,0:T(8,128)S(1)} collective-permute-done((f32[96,768]{1,0:T(8,128)}, f32[96,768]{1,0:T(8,128)S(1)}, u32[]{:S(2)}, u32[]{:S(2)}) %collective-permute-start.10) | collective-permute-done | bytes 294944 | tf_op jit(solution)/shard_map/ppermute | solution.py:672
  24.8 1.7 collective-permute-start.11
  26.6 3.6 collective-permute-start.20
  30.2 5.6 collective-permute-done.5.refs_3_
  35.8 2.5 collective-permute-start.15
  38.3 1.5 collective-permute-start.6
  41.2 7.1 %collective-permute-done.6.refs_4_ = f32[96,768]{1,0:T(8,128)} collective-permute-done((f32[96,768]{1,0:T(8,128)S(1)}, f32[96,768]{1,0:T(8,128)}, u32[]{:S(2)}, u32[]{:S(2)}) %collective-permute-start.6) | collective-permute-done | bytes 294944 | tf_op jit(solution)/shard_map/ppermute | solution.py:609
  48.3 1.5 collective-permute-start.12
  49.8 4.7 collective-permute-done.1.refs_4_
  54.5 1.6 collective-permute-start.26
  56.1 24.0 %collective-permute-done.20.refs_5_ = f32[192,768]{1,0:T(8,128)S(1)} collective-permute-done((f32[192,768]{1,0:T(8,128)S(1)}, f32[192,768]{1,0:T(8,128)S(1)}, u32[]{:S(2)}, u32[]{:S(2)}) %collective-permute-start.20) | collective-permute-done | bytes 589856 | tf_op jit(solution)/shard_map/ppermute | solution.py:673
  82.2 23.1 %all-gather.1 = f32[4,1,1152]{2,1,0:T(1,128)S(1)} all-gather(f32[1,1,1152]{2,1,0:T(1,128)S(1)} %reshape.124), channel_id=2, replica_groups=mesh['tensor'=4,'inner'=4,'outer'=2] {'tensor'}, dimensions={0}, use_global_device_ids=true | all-gather | bytes 23040 | tf_op jit(solution)/shard_map/all_gather | solution.py:674
  107.5 1.6 collective-permute-start.7
  111.4 2.2 pad_maximum_fusion.3
  113.7 2.4 pad_maximum_fusion.2
  117.5 1.5 collective-permute-start.22
  119.8 4.0 collective-permute-done.2.refs_5_
  123.8 1.5 collective-permute-start.27
  126.1 1.7 collective-permute-done.9.refs_7_
  133.8 2.1 pad.11.pos_ref
  139.4 12.0 %enter.1 = (f32[8,272,768]{2,1,0:T(8,128)}, bf16[8,272,768]{2,1,0:T(8,128)(2,1)}, bf16[8,272,768]{2,1,0:T(8,128)(2,1)}) custom-call(bf16[261,8,768]{2,1,0:T(8,128)(2,1)} %bitcast.94, bf16[261,8,768]{2,1,0:T(8,128)(2,1)} %bitcast.95, f32[8,272,128]{2,1,0:T(8,128)} %broadcast_in_dim.34.flag_ref.refs_8_, f32[3,768]{1,0:T(4,128)} %pad_maximum_fusion.8.vec_ref, ...), custom_call_target="tpu_custom_call" | custom-call | tf_op jit(solution)/shard_map/enter/pallas_call | solution.py:103
  152.7 9.0 %collective-permute-done.17.refs_7_ = f32[2,192,768]{2,1,0:T(8,128)S(1)} collective-permute-done((f32[2,192,768]{2,1,0:T(8,128)}, f32[2,192,768]{2,1,0:T(8,128)S(1)}, u32[]{:S(2)}, u32[]{:S(2)}) %collective-permute-start.17) | collective-permute-done | bytes 1179680 | tf_op jit(solution)/shard_map/ppermute | solution.py:611
  163.2 15.6 %attention.5 = (f32[8,272,768]{2,1,0:T(8,128)}, bf16[8,272,768]{2,1,0:T(8,128)(2,1)}, f32[8,272,128]{2,1,0:T(8,128)}, bf16[8,272,256]{2,1,0:T(8,128)(2,1)}) custom-call(bf16[8,272,768]{2,1,0:T(8,128)(2,1)} %get-tuple-element.62.refs_1_.refs_0_, f32[1,768]{1,0:T(1,128)} %broadcast_in_dim.38.refs_1_, bf16[1024,768]{1,0:T(8,128)(2,1)} %copy-done), custom_call_target="tpu_custom_call" | custom-call | tf_op jit(solution)/shard_map/attention/pallas_call | solution.py:268
  180.6 16.5 %attention.4 = (f32[8,272,768]{2,1,0:T(8,128)}, bf16[8,272,768]{2,1,0:T(8,128)(2,1)}, f32[8,272,128]{2,1,0:T(8,128)}, bf16[1024,768]{1,0:T(8,128)(2,1)}) custom-call(s32[2]{0:T(128)} %pad_add_fusion.refs_0_, bf16[8,272,768]{2,1,0:T(8,128)(2,1)} %get-tuple-element.62.refs_1_.refs_0_, f32[1,768]{1,0:T(1,128)} %broadcast_in_dim.36.refs_2_, ...), custom_call_target="tpu_custom_call" | custom-call | tf_op jit(solution)/shard_map/attention/pallas_call | solution.py:268
  197.0 16.4 %attention.6 = (f32[8,272,768]{2,1,0:T(8,128)}, bf16[8,272,768]{2,1,0:T(8,128)(2,1)}, f32[8,272,128]{2,1,0:T(8,128)}, bf16[1024,768]{1,0:T(8,128)(2,1)}) custom-call(s32[2]{0:T(128)} %pad_add_fusion.refs_0_, bf16[8,272,768]{2,1,0:T(8,128)(2,1)} %get-tuple-element.62.refs_1_.refs_0_, f32[1,768]{1,0:T(1,128)} %broadcast_in_dim.37.refs_2_, ...), custom_call_target="tpu_custom_call" | custom-call | tf_op jit(solution)/shard_map/attention/pallas_call | solution.py:268
  213.5 20.8 %attention.7 = (f32[8,272,768]{2,1,0:T(8,128)}, bf16[8,272,768]{2,1,0:T(8,128)(2,1)}, f32[8,272,128]{2,1,0:T(8,128)}, bf16[1024,768]{1,0:T(8,128)(2,1)}, bf16[8,272,768]{2,1,0:T(8,128)(2,1)}) custom-call(s32[2]{0:T(128)} %pad_add_fusion.refs_0_, bf16[8,272,768]{2,1,0:T(8,128)(2,1)} %get-tuple-element.62.refs_1_.refs_0_, f32[1,768]{1,0:T(1,128)} %broadcast_in_dim.35.refs_2_, ...), custom_call_target="tpu_custom_call" | custom-call | tf_op jit(solution)/shard_map/attention/pallas_call | solution.py:268
  234.3 16.3 %mlp.5 = (f32[8,272,768]{2,1,0:T(8,128)}, f32[8,272,768]{2,1,0:T(8,128)}, bf16[8,272,768]{2,1,0:T(8,128)(2,1)}, bf16[8,272,768]{2,1,0:T(8,128)(2,1)}, bf16[8,272,768]{2,1,0:T(8,128)(2,1)}, /*index=5*/f32[8,768]{1,0:T(8,128)}) custom-call(bf16[8,272,768]{2,1,0:T(8,128)(2,1)} %get-tuple-element.67.refs_1_.refs_0_, ...), custom_call_target="tpu_custom_call" | custom-call | tf_op jit(solution)/shard_map/mlp/pallas_call | solution.py:563
  251.6 16.4 %mlp.4 = (f32[8,272,768]{2,1,0:T(8,128)}, f32[8,272,768]{2,1,0:T(8,128)}) custom-call(s32[2]{0:T(128)} %pad_add_fusion.refs_0_, bf16[8,272,768]{2,1,0:T(8,128)(2,1)} %get-tuple-element.67.refs_1_.refs_0_, bf16[8,272,768]{2,1,0:T(8,128)(2,1)} %get-tuple-element.68.refs_2_.refs_1_, f32[5,768]{1,0:T(8,128)} %stack.130.refs_3_.refs_2_, ...), custom_call_target="tpu_custom_call" | custom-call | tf_op jit(solution)/shard_map/mlp/pallas_call | solution.py:563
  268.1 18.9 %mlp.6 = (f32[8,272,768]{2,1,0:T(8,128)}, f32[8,272,768]{2,1,0:T(8,128)}) custom-call(s32[2]{0:T(128)} %pad_add_fusion.refs_0_, bf16[8,272,768]{2,1,0:T(8,128)(2,1)} %get-tuple-element.67.refs_1_.refs_0_, bf16[8,272,768]{2,1,0:T(8,128)(2,1)} %get-tuple-element.68.refs_2_.refs_1_, f32[5,768]{1,0:T(8,128)} %stack.130.refs_3_.refs_2_, ...), custom_call_target="tpu_custom_call" | custom-call | tf_op jit(solution)/shard_map/mlp/pallas_call | solution.py:563
  286.9 28.4 %mlp.7 = (bf16[261,8,768]{2,1,0:T(8,128)(2,1)}, f32[8,272,768]{2,1,0:T(8,128)}, bf16[8,272,768]{2,1,0:T(8,128)(2,1)}, f32[8,768]{1,0:T(8,128)}) custom-call(s32[2]{0:T(128)} %pad_add_fusion.refs_0_, bf16[8,272,768]{2,1,0:T(8,128)(2,1)} %get-tuple-element.67.refs_1_.refs_0_, bf16[8,272,768]{2,1,0:T(8,128)(2,1)} %get-tuple-element.68.refs_2_.refs_1_, ...), custom_call_target="tpu_custom_call" | custom-call | tf_op jit(solution)/shard_map/mlp/pallas_call | solution.py:563
  315.4 21.8 %attention_back.5 = (f32[8,272,768]{2,1,0:T(8,128)}, bf16[8,272,768]{2,1,0:T(8,128)(2,1)}, f32[8,256]{1,0:T(8,128)}) custom-call(bf16[8,272,768]{2,1,0:T(8,128)(2,1)} %get-tuple-element.77.refs_0_, bf16[1024,768]{1,0:T(8,128)(2,1)} %copy-done, bf16[8,272,768]{2,1,0:T(8,128)(2,1)} %get-tuple-element.87.refs_2_, f32[8,272,128]{2,1,0:T(8,128)} %get-tuple-element.88.refs_3_), custom_call_target="tpu_custom_call" | custom-call | tf_op jit(solution)/shard_map/attention_back/pallas_call | solution.py:407
  337.2 21.7 %attention_back.4.refs_4_ = f32[8,272,768]{2,1,0:T(8,128)} custom-call(bf16[8,272,768]{2,1,0:T(8,128)(2,1)} %get-tuple-element.77.refs_0_, bf16[1024,768]{1,0:T(8,128)(2,1)} %get-tuple-element.81.refs_1_, bf16[8,272,768]{2,1,0:T(8,128)(2,1)} %get-tuple-element.82.refs_2_, f32[8,272,128]{2,1,0:T(8,128)} %get-tuple-element.83.refs_3_), custom_call_target="tpu_custom_call" | custom-call | tf_op jit(solution)/shard_map/attention_back/pallas_call | solution.py:407
  358.9 22.1 %attention_back.6.refs_5_ = f32[8,272,768]{2,1,0:T(8,128)} custom-call(bf16[8,272,768]{2,1,0:T(8,128)(2,1)} %get-tuple-element.77.refs_0_, bf16[1024,768]{1,0:T(8,128)(2,1)} %get-tuple-element.84.refs_1_, bf16[8,272,768]{2,1,0:T(8,128)(2,1)} %get-tuple-element.85.refs_2_, f32[8,272,128]{2,1,0:T(8,128)} %get-tuple-element.86.refs_3_, ...), custom_call_target="tpu_custom_call" | custom-call | tf_op jit(solution)/shard_map/attention_back/pallas_call | solution.py:407
  381.0 31.3 %attention_back.7 = (f32[2088,768]{1,0:T(8,128)}, f32[272,768]{1,0:T(8,128)}, f32[8,768]{1,0:T(8,128)}) custom-call(bf16[8,272,768]{2,1,0:T(8,128)(2,1)} %get-tuple-element.77.refs_0_, bf16[1024,768]{1,0:T(8,128)(2,1)} %get-tuple-element.78.refs_1_, bf16[8,272,768]{2,1,0:T(8,128)(2,1)} %get-tuple-element.79.refs_2_, ...), custom_call_target="tpu_custom_call" | custom-call | tf_op jit(solution)/shard_map/attention_back/pallas_call | solution.py:407
  418.8 5.6 concatenate.68
  425.9 8.9 %weight_grads.2 = (f32[768,768]{1,0:T(8,128)}, f32[768,256]{1,0:T(8,128)}) custom-call(bf16[2176,768]{1,0:T(8,128)(2,1)} %bitcast.81, bf16[2176,768]{1,0:T(8,128)(2,1)} %bitcast.93, bf16[2176,768]{1,0:T(8,128)(2,1)} %bitcast.82, bf16[2176,256]{1,0:T(8,128)(2,1)} %bitcast.105), custom_call_target="tpu_custom_call" | custom-call | tf_op jit(solution)/shard_map/weight_grads/pallas_call | solution.py:587
  434.7 1.9 fusion.5
  436.6 2.0 pad_maximum_fusion.1
  438.7 10.8 %weight_grads.3 = (f32[768,768]{1,0:T(8,128)}, f32[768,768]{1,0:T(8,128)}) custom-call(bf16[2176,768]{1,0:T(8,128)(2,1)} %bitcast.80, bf16[2176,768]{1,0:T(8,128)(2,1)} %bitcast.91, bf16[2176,768]{1,0:T(8,128)(2,1)} %bitcast.92, bf16[2176,768]{1,0:T(8,128)(2,1)} %bitcast.90), custom_call_target="tpu_custom_call" | custom-call | tf_op jit(solution)/shard_map/weight_grads/pallas_call | solution.py:587
  449.4 5.1 pad_maximum_fusion
  456.4 2.8 all-reduce.8.cloned.1.call-done
  459.2 1.9 constant_dynamic-slice_fusion.1
  461.1 34.0 %reduce-scatter.4.cloned.1.call-done = f32[192,768]{1,0:T(8,128)} async-done(((f32[768,768]{1,0:T(8,128)}), f32[192,768]{1,0:T(8,128)}) %reduce-scatter.4.cloned.1.call-update) | async-done | bytes 589840 | tf_op jit(solution)/shard_map/reduce_scatter | solution.py:618
  495.1 50.6 %reduce-scatter.6.cloned.1.call-done = f32[192,1536]{1,0:T(8,128)} async-done(((f32[768,1536]{1,0:T(8,128)}), f32[192,1536]{1,0:T(8,128)}) %reduce-scatter.6.cloned.1.call-update) | async-done | bytes 1179664 | tf_op jit(solution)/shard_map/reduce_scatter | solution.py:618
  545.7 65.5 %all-reduce.10.cloned.1.call-done = (f32[273,192]{0,1:T(8,128)}, f32[192,768]{1,0:T(8,128)}, f32[192,1536]{1,0:T(8,128)}) async-done(((f32[273,192]{0,1:T(8,128)}, f32[192,768]{1,0:T(8,128)}, f32[192,1536]{1,0:T(8,128)}), (f32[273,192]{0,1:T(8,128)}, f32[192,768]{1,0:T(8,128)}, f32[192,1536]{1,0:T(8,128)})) %all-reduce.10.cloned.1.call-update) | async-done | bytes 1979152 | tf_op jit(solution)/shard_map/psum | solution.py:618
  (221 shorter events, 45.9 us)
Async XLA Ops:
  7.2 452.0 %all-reduce.8.cloned.1.call-start = ((), (), s32[]{:S(2)}) async-start(), calls=%async_computation.4 | async-start | bytes 1769472
  9.0 15.8 %collective-permute-start.10 = (f32[96,768]{1,0:T(8,128)}, f32[96,768]{1,0:T(8,128)S(1)}, u32[]{:S(2)}, u32[]{:S(2)}) collective-permute-start(f32[96,768]{1,0:T(8,128)} %fusion.4), channel_id=1, source_target_pairs={{0,8},{8,0},{16,24},{24,16},{1,9},{9,1},{17,25},{25,17},{2,10},{10... | collective-permute-start | bytes 884744 | tf_op jit(solution)/shard_map/ppermute | solution.py:672
  12.1 23.7 %collective-permute-start.5 = (f32[96,768]{1,0:T(8,128)}, f32[96,768]{1,0:T(8,128)S(1)}, u32[]{:S(2)}, u32[]{:S(2)}) collective-permute-start(f32[96,768]{1,0:T(8,128)} %fusion.4), channel_id=1, source_target_pairs={{0,16},{8,24},{16,0},{24,8},{1,17},{9,25},{17,1},{25,9},{2,18},{10... | collective-permute-start | bytes 884744 | tf_op jit(solution)/shard_map/ppermute | solution.py:672
  14.7 23.6 %collective-permute-start = (f32[96,768]{1,0:T(8,128)}, f32[96,768]{1,0:T(8,128)S(1)}, u32[]{:S(2)}, u32[]{:S(2)}) collective-permute-start(f32[96,768]{1,0:T(8,128)} %fusion.4), channel_id=1, source_target_pairs={{0,24},{8,16},{16,8},{24,0},{1,25},{9,17},{17,9},{25,1},{2,26},{10... | collective-permute-start | bytes 884744 | tf_op jit(solution)/shard_map/ppermute | solution.py:672
  15.3 91.1 %copy-start.2 = (bf16[768,768]{0,1:T(8,128)(2,1)}, bf16[768,768]{0,1:T(8,128)(2,1)S(1)}, u32[]{:S(2)}) copy-start(bf16[768,768]{0,1:T(8,128)(2,1)S(1)} %copy.68) | copy-start | bytes 3538948
  15.3 66.8 %copy-start.40 = (f32[2,192]{1,0:T(2,128)S(1)}, f32[2,192]{1,0:T(2,128)}, u32[]{:S(2)}) copy-start(f32[2,192]{1,0:T(2,128)} %param.27) | copy-start | bytes 4612
  15.3 66.9 %copy-start.30 = (f32[768]{0:T(1024)S(1)}, f32[768]{0:T(1024)}, u32[]{:S(2)}) copy-start(f32[768]{0:T(1024)} %param.34) | copy-start | bytes 9220
  24.8 81.5 %copy-start.9 = (f32[96,768]{1,0:T(8,128)}, f32[96,768]{1,0:T(8,128)S(1)}, u32[]{:S(2)}) copy-start(f32[96,768]{1,0:T(8,128)S(1)} %collective-permute-done.10.refs_3_) | copy-start | bytes 884740
  24.8 14.9 %collective-permute-start.11 = (f32[96,768]{1,0:T(8,128)S(1)}, f32[96,768]{1,0:T(8,128)S(1)}, u32[]{:S(2)}, u32[]{:S(2)}) collective-permute-start(f32[96,768]{1,0:T(8,128)S(1)} %collective-permute-done.10.refs_3_), channel_id=1, source_target_pairs={{0,4},{1,5},{2,3},{3,2},{4,0},{5,1},{6,7},{7,6},{8,12},{9,13},{10,... | collective-permute-start | bytes 884744 | tf_op jit(solution)/shard_map/ppermute | solution.py:609
  26.5 28.0 %collective-permute-start.25 = (f32[192,768]{1,0:T(8,128)S(1)}, f32[192,768]{1,0:T(8,128)S(1)}, u32[]{:S(2)}, u32[]{:S(2)}) collective-permute-start(f32[192,768]{1,0:T(8,128)S(1)} %maximum_convert_fusion), channel_id=1, source_target_pairs={{0,8},{8,0},{16,24},{24,16},{1,9},{9,1},{17,25},{25,17},{2,10},{10... | collective-permute-start | bytes 1769480 | tf_op jit(solution)/shard_map/ppermute | solution.py:673
  26.6 53.5 %collective-permute-start.20 = (f32[192,768]{1,0:T(8,128)S(1)}, f32[192,768]{1,0:T(8,128)S(1)}, u32[]{:S(2)}, u32[]{:S(2)}) collective-permute-start(f32[192,768]{1,0:T(8,128)S(1)} %maximum_convert_fusion), channel_id=1, source_target_pairs={{0,16},{8,24},{16,0},{24,8},{1,17},{9,25},{17,1},{25,9},{2,18},{10... | collective-permute-start | bytes 1769480 | tf_op jit(solution)/shard_map/ppermute | solution.py:673
  35.8 71.7 %copy-start.10 = (f32[96,768]{1,0:T(8,128)}, f32[96,768]{1,0:T(8,128)S(1)}, u32[]{:S(2)}) copy-start(f32[96,768]{1,0:T(8,128)S(1)} %collective-permute-done.5.refs_3_) | copy-start | bytes 884740
  35.8 45.8 %collective-permute-start.15 = (f32[192,768]{1,0:T(8,128)S(1)}, f32[192,768]{1,0:T(8,128)}, u32[]{:S(2)}, u32[]{:S(2)}) collective-permute-start(f32[192,768]{1,0:T(8,128)S(1)} %maximum_convert_fusion), channel_id=1, source_target_pairs={{0,24},{8,16},{16,8},{24,0},{1,25},{9,17},{17,9},{25,1},{2,26},{10... | collective-permute-start | bytes 1769480 | tf_op jit(solution)/shard_map/ppermute | solution.py:673
  38.3 10.0 %collective-permute-start.6 = (f32[96,768]{1,0:T(8,128)S(1)}, f32[96,768]{1,0:T(8,128)}, u32[]{:S(2)}, u32[]{:S(2)}) collective-permute-start(f32[96,768]{1,0:T(8,128)S(1)} %collective-permute-done.5.refs_3_), channel_id=1, source_target_pairs={{0,4},{1,5},{2,3},{3,2},{4,0},{5,1},{6,7},{7,6},{8,12},{9,13},{10,... | collective-permute-start | bytes 884744 | tf_op jit(solution)/shard_map/ppermute | solution.py:609
  39.8 14.7 %collective-permute-start.1 = (f32[96,768]{1,0:T(8,128)S(1)}, f32[96,768]{1,0:T(8,128)S(1)}, u32[]{:S(2)}, u32[]{:S(2)}) collective-permute-start(f32[96,768]{1,0:T(8,128)S(1)} %collective-permute-done.refs_3_), channel_id=1, source_target_pairs={{0,4},{1,5},{2,3},{3,2},{4,0},{5,1},{6,7},{7,6},{8,12},{9,13},{10,... | collective-permute-start | bytes 884744 | tf_op jit(solution)/shard_map/ppermute | solution.py:609
  48.3 59.2 %collective-permute-start.12 = (f32[2,96,768]{2,1,0:T(8,128)}, f32[2,96,768]{2,1,0:T(8,128)}, u32[]{:S(2)}, u32[]{:S(2)}) collective-permute-start(f32[2,96,768]{2,1,0:T(8,128)} %pad_maximum_fusion.7), channel_id=1, source_target_pairs={{0,1},{1,0},{2,6},{3,7},{4,5},{5,4},{6,2},{7,3},{8,9},{9,8},{10,14... | collective-permute-start | bytes 1769480 | tf_op jit(solution)/shard_map/ppermute | solution.py:611
  54.5 25.6 %copy-start.16 = (f32[96,768]{1,0:T(8,128)}, f32[96,768]{1,0:T(8,128)S(1)}, u32[]{:S(2)}) copy-start(f32[96,768]{1,0:T(8,128)S(1)} %collective-permute-done.1.refs_4_) | copy-start | bytes 884740
  54.5 54.6 %collective-permute-start.13 = (f32[2,96,768]{2,1,0:T(8,128)}, f32[2,96,768]{2,1,0:T(8,128)}, u32[]{:S(2)}, u32[]{:S(2)}) collective-permute-start(f32[2,96,768]{2,1,0:T(8,128)} %pad_maximum_fusion.7), channel_id=1, source_target_pairs={{0,2},{1,3},{2,0},{3,1},{4,6},{5,7},{6,4},{7,5},{8,10},{9,11},{10,... | collective-permute-start | bytes 1769480 | tf_op jit(solution)/shard_map/ppermute | solution.py:612
  54.5 56.8 %copy-start.4 = (f32[192,768]{1,0:T(8,128)}, f32[192,768]{1,0:T(8,128)S(1)}, u32[]{:S(2)}) copy-start(f32[192,768]{1,0:T(8,128)S(1)} %collective-permute-done.25.refs_5_) | copy-start | bytes 1769476
  54.5 54.6 %collective-permute-start.26 = (f32[192,768]{1,0:T(8,128)S(1)}, f32[192,768]{1,0:T(8,128)S(1)}, u32[]{:S(2)}, u32[]{:S(2)}) collective-permute-start(f32[192,768]{1,0:T(8,128)S(1)} %collective-permute-done.25.refs_5_), channel_id=1, source_target_pairs={{0,4},{1,5},{2,3},{3,2},{4,0},{5,1},{6,7},{7,6},{8,12},{9,13},{10,... | collective-permute-start | bytes 1769480 | tf_op jit(solution)/shard_map/ppermute | solution.py:609
  80.1 31.3 %copy-start.5 = (f32[192,768]{1,0:T(8,128)}, f32[192,768]{1,0:T(8,128)S(1)}, u32[]{:S(2)}) copy-start(f32[192,768]{1,0:T(8,128)S(1)} %collective-permute-done.20.refs_5_) | copy-start | bytes 1769476
  80.1 29.6 %collective-permute-start.21 = (f32[192,768]{1,0:T(8,128)S(1)}, f32[192,768]{1,0:T(8,128)}, u32[]{:S(2)}, u32[]{:S(2)}) collective-permute-start(f32[192,768]{1,0:T(8,128)S(1)} %collective-permute-done.20.refs_5_), channel_id=1, source_target_pairs={{0,4},{1,5},{2,3},{3,2},{4,0},{5,1},{6,7},{7,6},{8,12},{9,13},{10,... | collective-permute-start | bytes 1769480 | tf_op jit(solution)/shard_map/ppermute | solution.py:609
  81.6 28.3 %collective-permute-start.16 = (f32[192,768]{1,0:T(8,128)}, f32[192,768]{1,0:T(8,128)}, u32[]{:S(2)}, u32[]{:S(2)}) collective-permute-start(f32[192,768]{1,0:T(8,128)} %collective-permute-done.15.refs_5_), channel_id=1, source_target_pairs={{0,4},{1,5},{2,3},{3,2},{4,0},{5,1},{6,7},{7,6},{8,12},{9,13},{10,... | collective-permute-start | bytes 1769480 | tf_op jit(solution)/shard_map/ppermute | solution.py:609
  107.5 9.9 %collective-permute-start.7 = (f32[2,96,768]{2,1,0:T(8,128)S(1)}, f32[2,96,768]{2,1,0:T(8,128)S(1)}, u32[]{:S(2)}, u32[]{:S(2)}) collective-permute-start(f32[2,96,768]{2,1,0:T(8,128)S(1)} %pad_maximum_fusion.6), channel_id=1, source_target_pairs={{0,1},{1,0},{2,6},{3,7},{4,5},{5,4},{6,2},{7,3},{8,9},{9,8},{10,14... | collective-permute-start | bytes 1769480 | tf_op jit(solution)/shard_map/ppermute | solution.py:611
  109.1 9.9 %collective-permute-start.8 = (f32[2,96,768]{2,1,0:T(8,128)S(1)}, f32[2,96,768]{2,1,0:T(8,128)S(1)}, u32[]{:S(2)}, u32[]{:S(2)}) collective-permute-start(f32[2,96,768]{2,1,0:T(8,128)S(1)} %pad_maximum_fusion.6), channel_id=1, source_target_pairs={{0,2},{1,3},{2,0},{3,1},{4,6},{5,7},{6,4},{7,5},{8,10},{9,11},{10,... | collective-permute-start | bytes 1769480 | tf_op jit(solution)/shard_map/ppermute | solution.py:612
  109.1 14.7 %collective-permute-start.2 = (f32[2,96,768]{2,1,0:T(8,128)S(1)}, f32[2,96,768]{2,1,0:T(8,128)S(1)}, u32[]{:S(2)}, u32[]{:S(2)}) collective-permute-start(f32[2,96,768]{2,1,0:T(8,128)S(1)} %pad_maximum_fusion.5), channel_id=1, source_target_pairs={{0,1},{1,0},{2,6},{3,7},{4,5},{5,4},{6,2},{7,3},{8,9},{9,8},{10,14... | collective-permute-start | bytes 1769480 | tf_op jit(solution)/shard_map/ppermute | solution.py:611
  109.7 15.6 %collective-permute-start.3 = (f32[2,96,768]{2,1,0:T(8,128)S(1)}, f32[2,96,768]{2,1,0:T(8,128)S(1)}, u32[]{:S(2)}, u32[]{:S(2)}) collective-permute-start(f32[2,96,768]{2,1,0:T(8,128)S(1)} %pad_maximum_fusion.5), channel_id=1, source_target_pairs={{0,2},{1,3},{2,0},{3,1},{4,6},{5,7},{6,4},{7,5},{8,10},{9,11},{10,... | collective-permute-start | bytes 1769480 | tf_op jit(solution)/shard_map/ppermute | solution.py:612
  109.9 15.9 %collective-permute-start.14 = (f32[2,96,768]{2,1,0:T(8,128)}, f32[2,96,768]{2,1,0:T(8,128)S(1)}, u32[]{:S(2)}, u32[]{:S(2)}) collective-permute-start(f32[2,96,768]{2,1,0:T(8,128)} %collective-permute-done.12.refs_5_), channel_id=1, source_target_pairs={{0,2},{1,3},{2,0},{3,1},{4,6},{5,7},{6,4},{7,5},{8,10},{9,11},{10,... | collective-permute-start | bytes 1769480 | tf_op jit(solution)/shard_map/ppermute | solution.py:613
  113.6 24.3 %copy-start.37 = (f32[768]{0:T(1024)S(1)}, f32[768]{0:T(1024)}, u32[]{:S(2)}) copy-start(f32[768]{0:T(1024)} %param.32) | copy-start | bytes 9220
  113.7 24.3 %copy-start.38 = (f32[768]{0:T(1024)S(1)}, f32[768]{0:T(1024)}, u32[]{:S(2)}) copy-start(f32[768]{0:T(1024)} %param.37) | copy-start | bytes 9220
  113.7 24.3 %copy-start.39 = (f32[768]{0:T(1024)S(1)}, f32[768]{0:T(1024)}, u32[]{:S(2)}) copy-start(f32[768]{0:T(1024)} %param.36) | copy-start | bytes 9220
  117.5 34.7 %collective-permute-start.22 = (f32[2,192,768]{2,1,0:T(8,128)}, f32[2,192,768]{2,1,0:T(8,128)}, u32[]{:S(2)}, u32[]{:S(2)}) collective-permute-start(f32[2,192,768]{2,1,0:T(8,128)} %pad_maximum_fusion.3), channel_id=1, source_target_pairs={{0,1},{1,0},{2,6},{3,7},{4,5},{5,4},{6,2},{7,3},{8,9},{9,8},{10,14... | collective-permute-start | bytes 3538952 | tf_op jit(solution)/shard_map/ppermute | solution.py:611
  119.0 33.3 %collective-permute-start.23 = (f32[2,192,768]{2,1,0:T(8,128)}, f32[2,192,768]{2,1,0:T(8,128)}, u32[]{:S(2)}, u32[]{:S(2)}) collective-permute-start(f32[2,192,768]{2,1,0:T(8,128)} %pad_maximum_fusion.3), channel_id=1, source_target_pairs={{0,2},{1,3},{2,0},{3,1},{4,6},{5,7},{6,4},{7,5},{8,10},{9,11},{10,... | collective-permute-start | bytes 3538952 | tf_op jit(solution)/shard_map/ppermute | solution.py:612
  123.8 27.7 %copy-start.18 = (f32[2,96,768]{2,1,0:T(8,128)}, f32[2,96,768]{2,1,0:T(8,128)S(1)}, u32[]{:S(2)}) copy-start(f32[2,96,768]{2,1,0:T(8,128)S(1)} %collective-permute-done.2.refs_5_) | copy-start | bytes 1769476
  123.8 28.0 %collective-permute-start.27 = (f32[2,192,768]{2,1,0:T(8,128)}, f32[2,192,768]{2,1,0:T(8,128)S(1)}, u32[]{:S(2)}, u32[]{:S(2)}) collective-permute-start(f32[2,192,768]{2,1,0:T(8,128)} %pad_maximum_fusion.4), channel_id=1, source_target_pairs={{0,1},{1,0},{2,6},{3,7},{4,5},{5,4},{6,2},{7,3},{8,9},{9,8},{10,14... | collective-permute-start | bytes 3538952 | tf_op jit(solution)/shard_map/ppermute | solution.py:611
  125.3 36.4 %collective-permute-start.17 = (f32[2,192,768]{2,1,0:T(8,128)}, f32[2,192,768]{2,1,0:T(8,128)S(1)}, u32[]{:S(2)}, u32[]{:S(2)}) collective-permute-start(f32[2,192,768]{2,1,0:T(8,128)} %pad_maximum_fusion.2), channel_id=1, source_target_pairs={{0,1},{1,0},{2,6},{3,7},{4,5},{5,4},{6,2},{7,3},{8,9},{9,8},{10,14... | collective-permute-start | bytes 3538952 | tf_op jit(solution)/shard_map/ppermute | solution.py:611
  125.8 2.0 collective-permute-start.9
  125.9 25.5 %copy-start.24 = (f32[1,768]{1,0:T(1,128)}, f32[1,768]{1,0:T(1,128)S(1)}, u32[]{:S(2)}) copy-start(f32[1,768]{1,0:T(1,128)S(1)} %stack.111.refs_9_) | copy-start | bytes 9220
  127.8 23.7 %collective-permute-start.4 = (f32[2,96,768]{2,1,0:T(8,128)S(1)}, f32[2,96,768]{2,1,0:T(8,128)}, u32[]{:S(2)}, u32[]{:S(2)}) collective-permute-start(f32[2,96,768]{2,1,0:T(8,128)S(1)} %collective-permute-done.2.refs_5_), channel_id=1, source_target_pairs={{0,2},{1,3},{2,0},{3,1},{4,6},{5,7},{6,4},{7,5},{8,10},{9,11},{10,... | collective-permute-start | bytes 1769480 | tf_op jit(solution)/shard_map/ppermute | solution.py:613
  151.6 116.5 %collective-permute-start.28 = (f32[2,192,768]{2,1,0:T(8,128)}, f32[2,192,768]{2,1,0:T(8,128)}, u32[]{:S(2)}, u32[]{:S(2)}) collective-permute-start(f32[2,192,768]{2,1,0:T(8,128)} %pad_maximum_fusion.4), channel_id=1, source_target_pairs={{0,2},{1,3},{2,0},{3,1},{4,6},{5,7},{6,4},{7,5},{8,10},{9,11},{10,... | collective-permute-start | bytes 3538952 | tf_op jit(solution)/shard_map/ppermute | solution.py:612
  151.8 45.3 %copy-start.8 = (f32[2,192,768]{2,1,0:T(8,128)}, f32[2,192,768]{2,1,0:T(8,128)S(1)}, u32[]{:S(2)}) copy-start(f32[2,192,768]{2,1,0:T(8,128)S(1)} %collective-permute-done.27.refs_7_) | copy-start | bytes 3538948
  151.8 135.2 %collective-permute-start.18 = (f32[2,192,768]{2,1,0:T(8,128)}, f32[2,192,768]{2,1,0:T(8,128)}, u32[]{:S(2)}, u32[]{:S(2)}) collective-permute-start(f32[2,192,768]{2,1,0:T(8,128)} %pad_maximum_fusion.2), channel_id=1, source_target_pairs={{0,2},{1,3},{2,0},{3,1},{4,6},{5,7},{6,4},{7,5},{8,10},{9,11},{10,... | collective-permute-start | bytes 3538952 | tf_op jit(solution)/shard_map/ppermute | solution.py:612
  152.1 115.9 %collective-permute-start.29 = (f32[2,192,768]{2,1,0:T(8,128)S(1)}, f32[2,192,768]{2,1,0:T(8,128)}, u32[]{:S(2)}, u32[]{:S(2)}) collective-permute-start(f32[2,192,768]{2,1,0:T(8,128)S(1)} %collective-permute-done.27.refs_7_), channel_id=1, source_target_pairs={{0,2},{1,3},{2,0},{3,1},{4,6},{5,7},{6,4},{7,5},{8,10},{9,11},{10,... | collective-permute-start | bytes 3538952 | tf_op jit(solution)/shard_map/ppermute | solution.py:613
  152.3 99.4 %collective-permute-start.24 = (f32[2,192,768]{2,1,0:T(8,128)}, f32[2,192,768]{2,1,0:T(8,128)}, u32[]{:S(2)}, u32[]{:S(2)}) collective-permute-start(f32[2,192,768]{2,1,0:T(8,128)} %collective-permute-done.22.refs_7_), channel_id=1, source_target_pairs={{0,2},{1,3},{2,0},{3,1},{4,6},{5,7},{6,4},{7,5},{8,10},{9,11},{10,... | collective-permute-start | bytes 3538952 | tf_op jit(solution)/shard_map/ppermute | solution.py:613
  161.7 125.2 %collective-permute-start.19 = (f32[2,192,768]{2,1,0:T(8,128)S(1)}, f32[2,192,768]{2,1,0:T(8,128)}, u32[]{:S(2)}, u32[]{:S(2)}) collective-permute-start(f32[2,192,768]{2,1,0:T(8,128)S(1)} %collective-permute-done.17.refs_7_), channel_id=1, source_target_pairs={{0,2},{1,3},{2,0},{3,1},{4,6},{5,7},{6,4},{7,5},{8,10},{9,11},{10,... | collective-permute-start | bytes 3538952 | tf_op jit(solution)/shard_map/ppermute | solution.py:613
  425.8 69.2 %reduce-scatter.4.cloned.1.call-start = ((), (), s32[]{:S(2)}) async-start(), calls=%async_computation.2 | async-start | bytes 2949120 | tf_op jit(solution)/shard_map/reduce_scatter | solution.py:618
  438.6 107.0 %reduce-scatter.6.cloned.1.call-start = ((), (), s32[]{:S(2)}) async-start(), calls=%async_computation.3 | async-start | bytes 5898240 | tf_op jit(solution)/shard_map/reduce_scatter | solution.py:618
  454.6 156.6 %all-reduce.10.cloned.1.call-start = ((), (), s32[]{:S(2)}) async-start(), calls=%async_computation.5 | async-start | bytes 4128768 | tf_op jit(solution)/shard_map/psum | solution.py:618
  (28 other events, 264.6 us)
Sparse Core Ops, SparseCore 0:
  426.0 33.2 all-reduce.7
  461.8 33.2 reduce-scatter.3
  497.8 47.8 reduce-scatter.5
  548.5 62.5 all-reduce.9

commit v2 on v1

--- a/solution.py
+++ b/solution.py
@@ -17,6 +17,7 @@
 MAIN = 256
 VMEM_LIMIT = 56 * 1024 * 1024
 PLANE = ("inner", "outer")
+PART = 96
 
 
 def mm_nt(a, b):
@@ -29,6 +30,30 @@
 
 def mm_tn(a, b):
     return lax.dot_general(a, b, (((0,), (0,)), ((), ())), preferred_element_type=F32)
+
+
+SHARE = 1.0
+
+
+def cost(us):
+    return pl.CostEstimate(flops=int(us * SHARE * 1.15e9), bytes_accessed=1 << 20, transcendentals=0)
+
+
+(
+    MASK_TOKEN,
+    PRE_ATTN_GAIN,
+    PRE_ATTN_BIAS,
+    PROJ_BIAS,
+    ATTN_SCALE,
+    PRE_MLP_GAIN,
+    PRE_MLP_BIAS,
+    FC2_BIAS,
+    MLP_SCALE,
+) = range(9)
+
+
+def row(ref, i):
+    return ref[i : i + 1, :]
 
 
 def params():
@@ -69,51 +94,88 @@
     return jnp.concatenate([ref[j, rows, :] for j in range(ref.shape[0])], 1)
 
 
-def enter_kernel(tok_ref, cot_ref, flag_ref, vec_ref, pos_ref, begin_ref, n1_ref, up_ref, tok_s, cot_s):
-    seq, crops, _ = tok_ref.shape
-    rows = pos_ref.shape[0]
+def flag_lanes(mask_ref, rows, prefix):
+    crop_mask = mask_ref[pl.ds(pl.program_id(0), 1), :]
+    patches = crop_mask.shape[1]
+    ones = jnp.broadcast_to((crop_mask == 1).astype(F32), (LANES, patches)).astype(BF16)
+    token = lax.broadcasted_iota(jnp.int32, (rows, patches), 0)
+    patch = lax.broadcasted_iota(jnp.int32, (rows, patches), 1)
+    return mm_nt((token == patch + prefix).astype(F32).astype(BF16), ones)
+
+
+def flag_wide(mask_ref, rows, prefix, width):
+    return jnp.concatenate([flag_lanes(mask_ref, rows, prefix)] * (width // LANES), 1) > 0.5
+
+
+def by_crop(src_ref, scratch):
+    seq, crops, _ = src_ref.shape
     step = 29 if seq % 29 == 0 else 1
 
     @pl.when(pl.program_id(0) == 0)
     def _():
         def move(i, carry):
-            part = pl.ds(i * step, step)
             dst = pl.ds(pl.multiple_of(i * (step * crops), crops), step * crops)
-            for src, out in ((tok_ref, tok_s), (cot_ref, cot_s)):
-                put_columns(out, dst, src[part].astype(F32).reshape(step * crops, -1))
+            put_columns(scratch, dst, src_ref[pl.ds(i * step, step)].astype(F32).reshape(step * crops, -1))
             return carry
 
         lax.fori_loop(0, seq // step, move, 0)
-        for out in (tok_s, cot_s):
-            out[:, seq * crops :, :] = jnp.zeros_like(out[:, seq * crops :, :])
-
-    mine = pl.ds(pl.program_id(0), rows, stride=crops)
-    flagged = flag_ref[0][:, 0:1] > 0.5
-    begin = jnp.where(flagged, vec_ref[0:1, :], get_columns(tok_s, mine)) + pos_ref[...]
+        scratch[:, seq * crops :, :] = jnp.zeros_like(scratch[:, seq * crops :, :])
+
+    return get_columns(scratch, pl.ds(pl.program_id(0), scratch.shape[1] // crops, stride=crops))
+
+
+def enter_kernel(tok_ref, mask_ref, vec_ref, pos_ref, begin_ref, n1_ref, scratch):
+    tok = by_crop(tok_ref, scratch)
+    rows = tok.shape[0]
+    near = pos_ref.shape[0] // 8 * 8
+    rest = pos_ref.shape[0] - near
+    pos = [pos_ref[0:near, :]]
+    if rest:
+        pos.append(jnp.concatenate([pos_ref[near:, :], jnp.zeros((8 - rest, tok.shape[1]), F32)], 0))
+    pos.append(jnp.zeros((rows - near - 8 * (rest > 0), tok.shape[1]), F32))
+    pos = jnp.concatenate(pos, 0)
+    prefix = tok_ref.shape[0] - mask_ref.shape[1]
+    flagged = flag_wide(mask_ref, rows, prefix, tok.shape[1])
+    begin = jnp.where(flagged, row(vec_ref, MASK_TOKEN), tok) + pos
     begin_ref[0] = begin
     xhat, _ = norm_parts(begin)
-    n1_ref[0] = (xhat * vec_ref[1:2, :] + vec_ref[2:3, :]).astype(BF16)
-    up_ref[0] = get_columns(cot_s, mine).astype(BF16)
-
-
-def enter(tok, cot, flags, vecs, pos):
+    n1_ref[0] = (xhat * row(vec_ref, PRE_ATTN_GAIN) + row(vec_ref, PRE_ATTN_BIAS)).astype(BF16)
+
+
+def enter(tok, mask, vecs, pos, rows):
     seq, crops, width = tok.shape
-    rows = pos.shape[0]
     shape = (crops, rows, width)
     return pl.pallas_call(
         enter_kernel,
         grid=(crops,),
-        in_specs=[whole(tok.shape), whole(cot.shape), block(flags.shape), whole(vecs.shape), whole(pos.shape)],
-        out_specs=[block(shape)] * 3,
-        out_shape=[
-            jax.ShapeDtypeStruct(shape, F32),
-            jax.ShapeDtypeStruct(shape, BF16),
-            jax.ShapeDtypeStruct(shape, BF16),
-        ],
-        scratch_shapes=[pltpu.VMEM((width // LANES, rows * crops, LANES), F32)] * 2,
+        in_specs=[whole(tok.shape), whole(mask.shape), whole(vecs.shape), whole(pos.shape)],
+        out_specs=[block(shape)] * 2,
+        out_shape=[jax.ShapeDtypeStruct(shape, F32), jax.ShapeDtypeStruct(shape, BF16)],
+        scratch_shapes=[pltpu.VMEM((width // LANES, rows * crops, LANES), F32)],
         compiler_params=params(),
+        cost_estimate=cost(7),
         name="enter",
-    )(tok, cot, flags, vecs, pos)
+    )(tok, mask, vecs, pos)
+
+
+def upstream_kernel(cot_ref, up_ref, scratch):
+    up_ref[0] = by_crop(cot_ref, scratch).astype(BF16)
+
+
+def upstream(cot, rows):
+    seq, crops, width = cot.shape
+    shape = (crops, rows, width)
+    return pl.pallas_call(
+        upstream_kernel,
+        grid=(crops,),
+        in_specs=[whole(cot.shape)],
+        out_specs=block(shape),
+        out_shape=jax.ShapeDtypeStruct(shape, BF16),
+        scratch_shapes=[pltpu.VMEM((width // LANES, rows * crops, LANES), F32)],
+        compiler_params=params(),
+        cost_estimate=cost(6),
+        name="upstream",
+    )(cot)
 
 
 def head_masks(heads):
@@ -169,116 +231,120 @@
     return mixed, log_total, attended, branch
 
 
+def take_pieces(it, count):
+    return [(ref, i) for ref in (next(it) for _ in range(count)) for i in range(ref.shape[0])]
+
+
 def place_pieces(info_ref, pieces, out_ref, base, first):
     p, core = info_ref[0], info_ref[1]
-    own, along, far, peer_a, peer_b = pieces
     q = p ^ 2
     a_bit = jnp.where(core == 0, 4, 1)
     b_bit = 5 - a_bit
-    spots = (
-        (own, None, p),
-        (along, None, p ^ a_bit),
-        (far, 0, p ^ b_bit),
-        (far, 1, p ^ 5),
-        (peer_a, 0, q),
-        (peer_a, 1, q ^ b_bit),
-        (peer_b, 0, q ^ a_bit),
-        (peer_b, 1, q ^ 5),
-    )
-    size = out_ref.shape[0]
-    for ref, slot, ident in spots:
-        view = ref if slot is None else ref.at[slot]
-        rows = 96
+    idents = (p, p ^ a_bit, p ^ b_bit, p ^ 5, q, q ^ b_bit, q ^ a_bit, q ^ 5)
+    for (ref, slot), ident in zip(pieces, idents, strict=True):
         dst = pl.multiple_of(first(ident), 32)
-        out_ref[pl.ds(dst, rows), :] = view[base : base + rows, :].astype(BF16)
-
-
-def attn_kernel(*refs, heads, tail_valid, gathered, accs, finish):
+        out_ref[pl.ds(dst, PART), :] = ref[slot, base : base + PART, :].astype(BF16)
+
+
+def attn_kernel(*refs, heads, tail_valid, own, into, accs, finish, gathers):
     it = iter(refs)
-    if gathered:
-        info = next(it)
-    n1_ref, bias_ref = next(it), next(it)
-    if gathered:
-        pieces = [next(it) for _ in range(5)]
+    if own:
+        n1_ref, bias_ref, qkv_ref, proj_ref = (next(it) for _ in range(4))
+        bias = bias_ref[...]
     else:
-        w_ref = next(it)
+        info, n1_ref = next(it), next(it)
+        pieces = take_pieces(it, gathers)
+        bias = pieces[0][0][0, PART : PART + 1, :]
     acc_refs = [next(it) for _ in range(accs)]
     if finish:
         begin_ref, vec_ref = next(it), next(it)
-    br_ref, mix_ref, lse_ref = next(it), next(it), next(it)
-    if gathered:
-        w_ref = next(it)
-
-        @pl.when(pl.program_id(0) == 0)
-        def _():
-            for i in range(4):
-                w_ref[i * WIDE + 192 : (i + 1) * WIDE, :] = jnp.zeros((WIDE - 192, w_ref.shape[1]), BF16)
-            place_pieces(info, pieces, w_ref, 0, lambda i: (i >> 1) * WIDE + (i & 1) * 96)
-
-    if not gathered:
-        att_ref = next(it)
-    mixed, log_total, attended, branch = attention_forward(
-        n1_ref[0], w_ref, bias_ref[...], heads, tail_valid
-    )
+    for _ in range(into):
+        next(it)
+    br_ref, mix_ref, lse_ref, w_ref = (next(it) for _ in range(4))
+
+    @pl.when(pl.program_id(0) == 0)
+    def _():
+        width = heads * HEAD_DIM
+        for i in range(4):
+            w_ref[i * WIDE + width : (i + 1) * WIDE, :] = jnp.zeros((WIDE - width, w_ref.shape[1]), BF16)
+        if own:
+            for i in range(3):
+                w_ref[i * WIDE : i * WIDE + width, :] = qkv_ref[i * width : (i + 1) * width, :]
+            w_ref[3 * WIDE : 3 * WIDE + width, :] = proj_ref[...]
+        else:
+            place_pieces(info, pieces, w_ref, 0, lambda i: (i >> 1) * WIDE + (i & 1) * PART)
+
+    mixed, log_total, attended, branch = attention_forward(n1_ref[0], w_ref, bias, heads, tail_valid)
     mix_ref[0] = mixed
     lse_ref[0] = log_total
-    if not gathered:
-        att_ref[0] = attended
+    if own:
+        next(it)[0] = attended
     for ref in acc_refs:
         branch = branch + ref[0]
     br_ref[0] = branch
     if finish:
         n2_ref = next(it)
-        middle = begin_ref[0] + vec_ref[0:1, :] * (branch + vec_ref[1:2, :])
+        middle = begin_ref[0] + row(vec_ref, ATTN_SCALE) * (branch + row(vec_ref, PROJ_BIAS))
         xhat, _ = norm_parts(middle)
-        n2_ref[0] = (xhat * vec_ref[2:3, :] + vec_ref[3:4, :]).astype(BF16)
-
-
-def attn(n1, bias, weights, info, accs, heads, tail_valid, finish=None):
+        n2_ref[0] = (xhat * row(vec_ref, PRE_MLP_GAIN) + row(vec_ref, PRE_MLP_BIAS)).astype(BF16)
+
+
+def attn(n1, weights, info, accs, heads, tail_valid, finish=None, span=None, into=()):
     crops, rows, width = n1.shape
-    gathered = info is not None
+    own = info is None
+    lo, hi = span or (0, crops)
     args, specs = [], []
+
+    def crop(shape):
+        return pl.BlockSpec((1,) + tuple(shape[1:]), lambda c: (c + lo,) + (0,) * (len(shape) - 1))
 
     def add(x, spec):
         args.append(x)
         specs.append(spec)
 
-    if gathered:
+    if not own:
         add(info, pl.BlockSpec(memory_space=pltpu.SMEM))
-    add(n1, block(n1.shape))
-    add(bias, whole(bias.shape))
+    add(n1, crop(n1.shape))
     for w in weights:
         add(w, whole(w.shape))
     for a in accs:
-        add(a, block(a.shape))
+        add(a, crop(a.shape))
     if finish is not None:
-        add(finish[0], block(finish[0].shape))
+        add(finish[0], crop(finish[0].shape))
         add(finish[1], whole(finish[1].shape))
     outs = [
-        ((crops, rows, width), F32, block),
-        ((crops, rows, 3 * WIDE), BF16, block),
-        ((crops, rows, LANES), F32, block),
+        ((crops, rows, width), F32, crop),
+        ((crops, rows, 3 * WIDE), BF16, crop),
+        ((crops, rows, LANES), F32, crop),
+        ((4 * WIDE, width), BF16, whole),
     ]
-    if gathered:
-        outs.append(((4 * WIDE, width), BF16, whole))
-    else:
-        outs.append(((crops, rows, WIDE), BF16, block))
+    if own:
+        outs.append(((crops, rows, WIDE), BF16, crop))
     if finish is not None:
-        outs.append(((crops, rows, width), BF16, block))
+        outs.append(((crops, rows, width), BF16, crop))
+    aliases = {}
+    for i, x in enumerate(into):
+        if outs[i][2] is crop:
+            aliases[len(args)] = i
+            add(x, pl.BlockSpec(memory_space=pl.ANY))
     return pl.pallas_call(
         functools.partial(
             attn_kernel,
             heads=heads,
             tail_valid=tail_valid,
-            gathered=gathered,
+            own=own,
+            gathers=len(weights),
+            into=len(aliases),
             accs=len(accs),
             finish=finish is not None,
         ),
-        grid=(crops,),
+        grid=(hi - lo,),
         in_specs=specs,
         out_specs=[kind(shape) for shape, _, kind in outs],
         out_shape=[jax.ShapeDtypeStruct(shape, dtype) for shape, dtype, _ in outs],
+        input_output_aliases=aliases,
         compiler_params=params(),
+        cost_estimate=cost((21 if finish is not None else 16) * (hi - lo) / crops),
         name="attention",
     )(*args)
 
@@ -333,7 +399,8 @@
     gb_ref, w_ref, mix_ref, lse_ref = (next(it) for _ in range(4))
     acc_refs = [next(it) for _ in range(accs)]
     if finish:
-        begin_ref, gmid_ref, flag_ref, vec_ref = (next(it) for _ in range(4))
+        info, begin_ref, gmid_ref, mask_ref, vec_ref = (next(it) for _ in range(5))
+        mid_ref, hsum_ref, qsum_ref = (next(it) for _ in range(3))
     else:
         gn_ref = next(it)
     first = pl.program_id(0) == 0
@@ -350,37 +417,47 @@
     if not finish:
         gn_ref[0] = gn
         return
-    gtok_ref, gpos_ref, sum_ref, gtok_s = (next(it) for _ in range(4))
+    gtok_ref, keep_ref, give_ref, gtok_s, pack = (next(it) for _ in range(5))
     xhat, rstd = norm_parts(begin_ref[0])
-    grad_begin = gmid_ref[0] + norm_back(xhat, rstd, gn, vec_ref[0:1, :])
-    flagged = flag_ref[0][:, 0:1] > 0.5
+    grad_begin = gmid_ref[0] + norm_back(xhat, rstd, gn, row(vec_ref, PRE_ATTN_GAIN))
+    rows, width = grad_begin.shape
+    seq = gtok_ref.shape[0] // 8
+    flagged = flag_wide(mask_ref, rows, seq - mask_ref.shape[1], width)
     cleared = jnp.where(flagged, 0.0, grad_begin)
-    seq = gtok_ref.shape[0] // 8
-    put_columns(gtok_s, pl.ds(pl.program_id(0), cleared.shape[0], stride=8), cleared)
-    sums = jnp.concatenate(
-        [
-            row_sum(gn * xhat),
-            row_sum(gn),
-            row_sum(grad_begin - cleared),
-            jnp.zeros((5, gn.shape[1]), F32),
-        ],
-        0,
-    )
+    put_columns(gtok_s, pl.ds(pl.program_id(0), rows, stride=8), cleared)
+    last = rows + 8
+    sums = jnp.concatenate([row_sum(gn * xhat), row_sum(gn), row_sum(grad_begin - cleared)], 0)
 
     @pl.when(first)
     def _():
-        sum_ref[...] = sums
-        gpos_ref[...] = grad_begin
+        pack[0:rows, :] = grad_begin
+        pack[last : last + 3, :] = sums
 
     @pl.when(jnp.logical_not(first))
     def _():
-        sum_ref[...] += sums
-        gpos_ref[...] += grad_begin
+        pack[0:rows, :] += grad_begin
+        pack[last : last + 3, :] += sums
 
     @pl.when(pl.program_id(0) == pl.num_programs(0) - 1)
     def _():
         for j in range(gtok_s.shape[0]):
             gtok_ref[:, j * LANES : (j + 1) * LANES] = gtok_s[j, 0 : seq * 8, :]
+        pack[rows:last, :] = mid_ref[...]
+        pack[last + 3 : last + 4, :] = hsum_ref[0:1, :]
+        quarter = keep_ref.shape[2]
+        small = heads * HEAD_DIM // 4
+        for i in range(4):
+            part = pack[:, i * quarter : (i + 1) * quarter]
+
+            def put(ref):
+                ref[i // 2] = part
+                for t in range(2):
+                    ref[i // 2, last + 4 + t : last + 5 + t, 0:small] = qsum_ref[
+                        t : t + 1, i * small : (i + 1) * small
+                    ]
+
+            pl.when(info[1] == i % 2)(functools.partial(put, keep_ref))
+            pl.when(info[1] != i % 2)(functools.partial(put, give_ref))
 
 
 def attn_back(gb, w, mixed, lse, accs, heads, tail_valid, own=False, finish=None, seq=None):
@@ -390,10 +467,12 @@
     specs += [block(a.shape) for a in accs]
     outs, scratch = [], []
     if finish is not None:
-        begin, gmid, flags, vecs = finish
-        args += [begin, gmid, flags, vecs]
-        specs += [block(begin.shape), block(gmid.shape), block(flags.shape), whole(vecs.shape)]
+        info, begin, gmid, *tables = finish
+        args += [info, begin, gmid, *tables]
+        specs += [pl.BlockSpec(memory_space=pltpu.SMEM), block(begin.shape), block(gmid.shape)]
+        specs += [whole(x.shape) for x in tables]
         scratch.append(pltpu.VMEM((width // LANES, rows * crops, LANES), F32))
+        scratch.append(pltpu.VMEM((rows + 16, width), F32))
     else:
         outs.append(((crops, rows, width), F32, block))
     if own:
@@ -401,8 +480,8 @@
     if finish is not None:
         outs += [
             ((seq * crops, width), F32, whole),
-            ((rows, width), F32, whole),
-            ((8, width), F32, whole),
+            ((2, rows + 16, width // 4), F32, whole),
+            ((2, rows + 16, width // 4), F32, whole),
         ]
     return pl.pallas_call(
         functools.partial(
@@ -419,6 +498,7 @@
         out_shape=[jax.ShapeDtypeStruct(shape, dtype) for shape, dtype, _ in outs],
         scratch_shapes=scratch,
         compiler_params=params(),
+        cost_estimate=cost(31 if finish is not None else 22),
         name="attention_back",
     )(*args)
 
@@ -433,11 +513,13 @@
     it = iter(refs)
     if gathered:
         info = next(it)
-    n2_ref, up_ref, vec_ref, bias_ref = (next(it) for _ in range(4))
+    n2_ref, up_ref, vec_ref = (next(it) for _ in range(3))
     if gathered:
-        pieces = [next(it) for _ in range(5)]
+        pieces = take_pieces(it, 4)
+        bias = pieces[0][0][0, PART : PART + 1, :]
     else:
-        w1_ref, w2_ref = next(it), next(it)
+        bias_ref, w1_ref, w2_ref = (next(it) for _ in range(3))
+        bias = bias_ref[...]
     acc_refs = [(next(it), next(it)) for _ in range(accs)]
     if finish:
         begin_ref, br_ref = next(it), next(it)
@@ -454,14 +536,14 @@
 
         @pl.when(first)
         def _():
-            place_pieces(info, pieces, w1_ref, 0, lambda i: i * 96)
-            place_pieces(info, pieces, w2_ref, 96, lambda i: i * 96)
+            place_pieces(info, pieces, w1_ref, 0, lambda i: i * PART)
+            place_pieces(info, pieces, w2_ref, PART + 8, lambda i: i * PART)
 
     up = up_ref[0].astype(F32)
-    grad_output = up * vec_ref[0:1, :]
+    grad_output = up * row(vec_ref, MLP_SCALE)
     go = grad_output.astype(BF16)
     n2 = n2_ref[0]
-    a, slope = gelu_and_slope(mm_nt(n2, w1_ref[...]) + bias_ref[...])
+    a, slope = gelu_and_slope(mm_nt(n2, w1_ref[...]) + bias)
     a = a.astype(BF16)
     gh = mm_nt(go, w2_ref[...]) * slope
     if own:
@@ -481,16 +563,16 @@
         out_ref[0] = out
         gn_ref[0] = gn
         return
-    mlp_scale, fc2_bias, attn_scale, proj_bias, gain = (vec_ref[i : i + 1, :] for i in range(5))
-    out = out + fc2_bias
-    branch = br_ref[0] + proj_bias
+    out = out + row(vec_ref, FC2_BIAS)
+    branch = br_ref[0] + row(vec_ref, PROJ_BIAS)
+    attn_scale = row(vec_ref, ATTN_SCALE)
     middle = begin_ref[0] + attn_scale * branch
-    result = middle + mlp_scale * out
+    result = middle + row(vec_ref, MLP_SCALE) * out
     rows = result.shape[0]
     crops = 8
     put_columns(res_s, pl.ds(pl.program_id(0), rows, stride=crops), result)
     xhat, rstd = norm_parts(middle)
-    gmid = up + norm_back(xhat, rstd, gn, gain)
+    gmid = up + norm_back(xhat, rstd, gn, row(vec_ref, PRE_MLP_GAIN))
     gmid_ref[0] = gmid
     gbr = gmid * attn_scale
     gb_ref[0] = gbr.astype(BF16)
@@ -521,9 +603,8 @@
         lax.fori_loop(0, seq // step, move, 0)
 
 
-def mlp(n2, up, vecs, bias, weights, info, accs, own=False, finish=None, seq=None):
+def mlp(n2, up, vecs, weights, info, accs, hidden, own=False, finish=None, seq=None):
     crops, rows, width = n2.shape
-    hidden = bias.shape[1]
     gathered = info is not None
     args, specs = [], []
 
@@ -536,7 +617,6 @@
     add(n2, block(n2.shape))
     add(up, block(up.shape))
     add(vecs, whole(vecs.shape))
-    add(bias, whole(bias.shape))
     for w in weights:
         add(w, whole(w.shape))
     for pair in accs:
@@ -568,29 +648,28 @@
         out_shape=[jax.ShapeDtypeStruct(shape, dtype) for shape, dtype, _ in outs],
         scratch_shapes=scratch,
         compiler_params=params(),
+        cost_estimate=cost(28 if finish is not None else 17),
         name="mlp",
     )(*args)
 
 
-def weight_grad_kernel(x1_ref, y1_ref, x2_ref, y2_ref, o1_ref, o2_ref):
-    o1_ref[...] = mm_tn(x1_ref[...], y1_ref[...])
-    o2_ref[...] = mm_tn(x2_ref[...], y2_ref[...])
-
-
-def weight_grads(x1, y1, x2, y2):
+def weight_grad_kernel(x1_ref, y1_ref, x2_ref, y2_ref, out_ref, *, parts):
+    first, second = mm_tn(x1_ref[...], y1_ref[...]), mm_tn(x2_ref[...], y2_ref[...])
+    out_ref[...] = jnp.concatenate([(first, second)[i][:, lo:hi] for i, lo, hi in parts], 1)
+
+
+def weight_grads(x1, y1, x2, y2, parts):
     rows, width = x1.shape
     col = pl.BlockSpec((rows, WIDE), lambda i: (0, i))
-
-    def out(y):
-        return pl.BlockSpec((WIDE, y.shape[1]), lambda i: (i, 0))
-
+    wide = sum(hi - lo for _, lo, hi in parts)
     return pl.pallas_call(
-        weight_grad_kernel,
+        functools.partial(weight_grad_kernel, parts=parts),
         grid=(width // WIDE,),
         in_specs=[col, whole(y1.shape), col, whole(y2.shape)],
-        out_specs=[out(y1), out(y2)],
-        out_shape=[jax.ShapeDtypeStruct((width, y.shape[1]), F32) for y in (y1, y2)],
+        out_specs=pl.BlockSpec((WIDE, wide), lambda i: (i, 0)),
+        out_shape=jax.ShapeDtypeStruct((width, wide), F32),
         compiler_params=params(),
+        cost_estimate=cost(10),
         name="weight_grads",
     )(x1, y1, x2, y2)
 
@@ -604,18 +683,41 @@
     return pairs
 
 
-def spread(piece, perms):
-    one, two, three = perms
-    along = lax.ppermute(piece, PLANE, one)
-    both = jnp.stack([piece, along])
-    far = lax.ppermute(both, PLANE, two)
-    peer_a = lax.ppermute(both, PLANE, three)
-    peer_b = lax.ppermute(far, PLANE, three)
-    return [piece, along, far, peer_a, peer_b]
-
-
-def reduce_inner(x):
-    return lax.psum(lax.psum_scatter(x, "inner", scatter_dimension=0, tiled=True), "outer")
+def after(x, *others):
+    return lax.optimization_barrier((x, *others))[0] if others else x
+
+
+def fence(new, *done):
+    return lax.optimization_barrier((*new, *done))[: len(new)]
+
+
+class PlaneSum:
+    def __init__(self, sizes, inner, keep, give):
+        _, self.inner_n, self.outer_n = sizes
+        self.side = inner // 2
+        self.keep, self.give = keep, give
+
+    def cores(self, *others):
+        self.one = lax.ppermute(
+            after(self.give, *others), "inner", [(i, i ^ 1) for i in range(self.inner_n)]
+        )
+        return self.one
+
+    def pick(self, side):
+        return sum(lax.dynamic_index_in_dim(x, side, 0, keepdims=False) for x in (self.keep, self.one))
+
+    def sides(self, *others):
+        give = after(self.pick(1 - self.side), *others)
+        self.two = lax.ppermute(give, "inner", [(i, i ^ 2) for i in range(self.inner_n)])
+        return self.two
+
+    def groups(self, *others):
+        total = self.pick(self.side) + after(self.two, *others)
+        k = 1
+        while k < self.outer_n:
+            total = total + lax.ppermute(total, "outer", [(o, o ^ k) for o in range(self.outer_n)])
+            k *= 2
+        return total
 
 
 def per_device(
@@ -654,135 +756,205 @@
     info = jnp.stack([place, inner % 2]).astype(jnp.int32)
 
     qkv_rows = qkv_weight.transpose(1, 2, 0).reshape(3 * head_width, width)
-    own_attn = jnp.concatenate([qkv_rows, proj_weight], 0)
     own_fc1 = fc1_weight.T
-    part = width // 8
 
     def eighth(x):
-        return lax.dynamic_slice_in_dim(x, place * part, part, 0).astype(F32)
-
-    attn_piece = eighth(own_attn)
-    mlp_piece = jnp.concatenate([eighth(own_fc1), eighth(fc2_weight)], 0)
+        return lax.dynamic_slice_in_dim(x, place * PART, PART, 0).astype(F32)
+
+    ones = jnp.ones((heads,), F32)
+    zeros = jnp.zeros((WIDE,), F32)
+    attn_bias = jnp.concatenate(
+        [qv_bias[0], zeros[head_width:], zeros, qv_bias[1], ones, zeros[head_width + heads :]]
+    )[None, :]
+    mlp_bias = fc1_bias[None, :]
+    below = jnp.zeros((7, width), F32)
+    attn_piece = jnp.concatenate(
+        [eighth(jnp.concatenate([qkv_rows, proj_weight], 0)), attn_bias, below], 0
+    )
+    fc1_piece = jnp.concatenate([eighth(own_fc1), mlp_bias, below], 0)
+    fc2_piece = eighth(fc2_weight)
     perms = (
         plane_perm(inner_n, outer_n, lambda i, o: (i, o ^ 1) if i % 2 else (i ^ 2, o)),
         plane_perm(inner_n, outer_n, lambda i, o: (i ^ 2, o) if i % 2 else (i, o ^ 1)),
         plane_perm(inner_n, outer_n, lambda i, o: (i ^ 1, o)),
     )
-    hops = [[(i, i ^ k) for i in range(tensor_n)] for k in range(1, tensor_n)]
-    attn_parts = [spread(lax.ppermute(attn_piece, "tensor", hop), perms) for hop in hops]
-    mlp_parts = [spread(lax.ppermute(mlp_piece, "tensor", hop), perms) for hop in hops]
-    all_biases = lax.all_gather(jnp.concatenate([qv_bias.reshape(-1), fc1_bias]), "tensor")
-
-    def biases_of(k):
-        one = lax.dynamic_index_in_dim(all_biases, t ^ k, 0, keepdims=False)
-        q_bias, v_bias = one[0:head_width], one[head_width : 2 * head_width]
-        ones = jnp.ones((heads,), F32)
-        gap = jnp.zeros((WIDE - head_width - heads,), F32)
-        zeros = jnp.zeros((WIDE,), F32)
-        row = jnp.concatenate([q_bias, zeros[head_width:], zeros, v_bias, ones, gap])
-        return row[None, :], one[2 * head_width :][None, :]
-
-    biases = [biases_of(k) for k in range(tensor_n)]
-
-    flag = jnp.concatenate(
+    def over_z(x, k):
+        return lax.ppermute(x, "tensor", [(i, i ^ k) for i in range(tensor_n)])
+
+    along, far, peer = (functools.partial(lax.ppermute, axis_name=PLANE, perm=p) for p in perms)
+
+    vecs = jnp.stack(
         [
-            jnp.zeros((crops, seq - patch_mask.shape[1]), F32),
-            (patch_mask == 1).astype(F32),
-            jnp.zeros((crops, rows - seq), F32),
-        ],
-        1,
-    )
-    flags = jnp.broadcast_to(flag[:, :, None], (crops, rows, LANES))
-    pos = jnp.pad(pos_embed, ((0, rows - seq), (0, 0)))
-    begin, n1, up = enter(
-        tokens.transpose(1, 0, 2),
-        cotangent.transpose(1, 0, 2),
-        flags,
-        jnp.stack([mask_token, pre_attn_gain, pre_attn_bias]),
-        pos,
-    )
-
-    gap_rows = jnp.zeros((WIDE - head_width, width), BF16)
-    own_w = jnp.concatenate(
-        sum(
-            ([own_attn[i * head_width : (i + 1) * head_width], gap_rows] for i in range(4)),
-            [],
-        ),
-        0,
-    )
-    attn_vecs = jnp.stack([attn_scale, proj_bias, pre_mlp_gain, pre_mlp_bias])
+            mask_token,
+            pre_attn_gain,
+            pre_attn_bias,
+            proj_bias,
+            attn_scale,
+            pre_mlp_gain,
+            pre_mlp_bias,
+            fc2_bias,
+            mlp_scale,
+        ]
+    )
     run = functools.partial(attn, heads=heads, tail_valid=tail_valid)
-    br0, mix0, lse0, att0 = run(n1, biases[0][0], [own_w], None, [])
-    br1, mix1, lse1, w_1 = run(n1, biases[1][0], attn_parts[0], info, [br0])
-    br2, mix2, lse2, w_2 = run(n1, biases[2][0], attn_parts[1], info, [])
-    br, mix3, lse3, w_3, n2 = run(
-        n1, biases[3][0], attn_parts[2], info, [br2, br1], finish=(begin, attn_vecs)
-    )
-
-    mlp_vecs = jnp.stack([mlp_scale, fc2_bias, attn_scale, proj_bias, pre_mlp_gain])
-    out0, gn0, a0, gh0, go0, hsum = mlp(
-        n2, up, mlp_vecs, biases[0][1], [own_fc1, fc2_weight], None, [], own=True
-    )
+    layer = functools.partial(mlp, hidden=hidden)
+
+    quarter = width // inner_n
+
+    def plane_sum(x):
+        x = x.reshape(2, 2, quarter, -1)
+        take = lambda core: lax.dynamic_index_in_dim(x, core, 1, keepdims=False)
+        return PlaneSum(sizes, inner, take(inner % 2), take(1 - inner % 2))
+
+    def pair(first, second):
+        return jnp.stack([first, second])
+
+    cut = 56
+    attn_hi, attn_lo = attn_piece[:cut], attn_piece[cut:]
+
+    a1, a2 = over_z(attn_piece, 1), over_z(attn_piece, 2)
+    begin, n1 = enter(tokens.transpose(1, 0, 2), patch_mask, vecs, pos_embed, rows)
+
+    n1, a1, a2, attn_hi, fc1_piece = fence((n1, a1, a2, attn_hi, fc1_piece))
+    b1, b2 = along(a1), along(a2)
+    a3_hi, m1_hi = over_z(attn_hi, 3), over_z(fc1_piece, 1)
+    half = crops // 2
+    own_w = [attn_bias, qkv_rows, proj_weight]
+    early = run(n1, own_w, None, [], span=(0, half))
+
+    both1 = pair(a1, b1)
+    cot, both1, attn_lo = fence(
+        (cotangent.transpose(1, 0, 2), both1, attn_lo), early[0], b1, b2, a3_hi, m1_hi
+    )
+    c1, d1 = far(both1), peer(both1)
+    a3_lo = over_z(attn_lo, 3)
+    up = upstream(cot, rows)
+
+    both2, a3 = pair(a2, b2), jnp.concatenate([a3_hi, a3_lo], 0)
+    n1, c1, both2, a3 = fence((n1, c1, both2, a3), up, d1)
+    e1 = peer(c1)
+    c2, d2 = far(both2), peer(both2)
+    b3 = along(a3)
+    br0, mix0, lse0, w_0, att0 = run(n1, own_w, None, [], span=(half, crops), into=early)
+
+    both3 = pair(a3, b3)
+    n1, c2, both3, fc1_piece, fc2_piece = fence(
+        (n1, c2, both3, fc1_piece, fc2_piece), br0, e1, d2
+    )
+    e2 = peer(c2)
+    c3 = far(both3)
+    m1_lo = over_z(fc2_piece, 1)
+    m2_hi = over_z(fc1_piece, 2)
+    br1, mix1, lse1, w_1 = run(n1, [both1, c1, d1, e1], info, [br0])
+
+    four3, m1 = jnp.concatenate([both3, c3], 0), jnp.concatenate([m1_hi, m1_lo], 0)
+    n1, four3, m1, fc2_piece = fence((n1, four3, m1, fc2_piece), br1, e2, m2_hi)
+    de3 = peer(four3)
+    f1 = along(m1)
+    m2_lo = over_z(fc2_piece, 2)
+    br2, mix2, lse2, w_2 = run(n1, [both2, c2, d2, e2], info, [])
+
+    two1, m2 = pair(m1, f1), jnp.concatenate([m2_hi, m2_lo], 0)
+    n1, two1, m2, fc1_piece = fence((n1, two1, m2, fc1_piece), br2, de3)
+    g1, h1 = far(two1), peer(two1)
+    f2 = along(m2)
+    m3_hi = over_z(fc1_piece, 3)
+    br, mix3, lse3, w_3, n2 = run(n1, [four3, de3], info, [br2, br1], finish=(begin, vecs))
+
+    two2 = pair(m2, f2)
+    n2, g1, two2, fc2_piece = fence((n2, g1, two2, fc2_piece), h1, m3_hi)
+    i1 = peer(g1)
+    g2, h2 = far(two2), peer(two2)
+    m3_lo = over_z(fc2_piece, 3)
+    out0, gn0, a0, gh0, go0, hsum = layer(
+        n2, up, vecs, [mlp_bias, own_fc1, fc2_weight], None, [], own=True
+    )
+
     flat = lambda x: x.reshape(crops * rows, -1)
-    grad_fc1, grad_fc2 = weight_grads(flat(n2), flat(gh0), flat(go0), flat(a0))
-    shares_mlp = reduce_inner(jnp.concatenate([grad_fc1, grad_fc2], 1))
-    acc1 = mlp(n2, up, mlp_vecs, biases[1][1], mlp_parts[0], info, [(out0, gn0)])
-    acc2 = mlp(n2, up, mlp_vecs, biases[2][1], mlp_parts[1], info, [])
-    result, gmid, gb, mid_sums = mlp(
-        n2, up, mlp_vecs, biases[3][1], mlp_parts[2], info, [acc2, acc1], finish=(begin, br), seq=seq
+    m3 = jnp.concatenate([m3_hi, m3_lo], 0)
+    n2, g2, m3 = fence((n2, g2, m3), out0, i1, h2)
+    i2 = peer(g2)
+    f3 = along(m3)
+    mlp_grads = weight_grads(
+        flat(n2), flat(gh0), flat(go0), flat(a0), ((0, 0, hidden), (1, 0, hidden))
+    )
+
+    two3 = pair(m3, f3)
+    n2, two3, mlp_grads = fence((n2, two3, mlp_grads), i2)
+    mlp_sum = plane_sum(mlp_grads)
+    s1 = mlp_sum.cores()
+    g3, h3 = far(two3), peer(two3)
+    acc1 = layer(n2, up, vecs, [two1, g1, h1, i1], info, [(out0, gn0)])
+
+    n2, g3 = fence((n2, g3), acc1[0], h3, s1)
+    s2 = mlp_sum.sides(acc1[0])
+    i3 = peer(g3)
+    acc2 = layer(n2, up, vecs, [two2, g2, h2, i2], info, [])
+
+    n2 = after(n2, i3)
+    result, gmid, gb, mid_sums = layer(
+        n2, up, vecs, [two3, g3, h3, i3], info, [acc2, acc1], finish=(begin, br), seq=seq
     )
 
     back = functools.partial(attn_back, heads=heads, tail_valid=tail_valid)
-    gn0, gm0, qv_sums = back(gb, own_w, mix0, lse0, [], own=True)
-    grad_qkv, grad_proj = weight_grads(flat(n1), flat(gm0), flat(gb), flat(att0))
-    pieces = [grad_qkv[:, i * WIDE : i * WIDE + head_width] for i in range(3)]
-    shares_attn = reduce_inner(jnp.concatenate(pieces + [grad_proj[:, :head_width]], 1))
+    s3 = mlp_sum.groups(gb)
+    gb = after(gb, s2)
+    gn0, gm0, qv_sums = back(gb, w_0, mix0, lse0, [], own=True)
+    attn_grads = weight_grads(
+        flat(n1),
+        flat(gm0),
+        flat(gb),
+        flat(att0),
+        tuple((0, i * WIDE, i * WIDE + head_width) for i in range(3)) + ((1, 0, head_width),),
+    )
+
+    gb = after(gb, attn_grads, s3)
+    attn_sum = plane_sum(attn_grads)
+    s1 = attn_sum.cores()
     (gn1,) = back(gb, w_1, mix1, lse1, [gn0])
+    gb = after(gb, s1, gn1)
+    s2 = attn_sum.sides(gn1)
     (gn2,) = back(gb, w_2, mix2, lse2, [])
-    gtok, gpos, last_sums = back(
-        gb, w_3, mix3, lse3, [gn2, gn1], finish=(begin, gmid, flags, pre_attn_gain[None, :]), seq=seq
-    )
-
-    quarter = width // inner_n
+    gb = after(gb, s2, gn2)
+    shares_attn = attn_sum.groups(gn2)
+    gtok, keep, give = back(
+        gb,
+        w_3,
+        mix3,
+        lse3,
+        [gn2, gn1],
+        finish=(info, begin, gmid, patch_mask, vecs, mid_sums, hsum, qv_sums),
+        seq=seq,
+    )
+    shares_mlp = s3
+
     small = head_width // inner_n
-
-    def spaced(x):
-        return jnp.pad(x.reshape(inner_n, small), ((0, 0), (0, quarter - small))).reshape(1, width)
-
-    pack = jnp.concatenate(
-        [
-            gpos[:seq],
-            mid_sums[0:6],
-            last_sums[0:3],
-            hsum[0:1],
-            spaced(qv_sums[0, :head_width]),
-            spaced(qv_sums[1, :head_width]),
-        ],
-        0,
-    )
-    pack = pack.reshape(-1, inner_n, quarter).transpose(1, 0, 2).reshape(-1, quarter)
-    small_sums = reduce_inner(pack)
-    vec = lambda i: small_sums[seq + i]
+    small_sum = PlaneSum(sizes, inner, keep, after(give, shares_attn))
+    small_sum.cores()
+    small_sum.sides()
+    small_sums = small_sum.groups()
+    mid = lambda i: small_sums[rows + i]
+    vec = lambda i: small_sums[rows + 8 + i]
     grad_qkv = shares_attn[:, : 3 * head_width].reshape(-1, 3, head_width)
     return (
         result.transpose(1, 0, 2),
         gtok.reshape(seq, crops, width).transpose(1, 0, 2),
-        vec(8),
+        vec(2),
         small_sums[:seq],
-        vec(6),
-        vec(7),
+        vec(0),
+        vec(1),
         grad_qkv,
-        jnp.stack([vec(10)[:small], vec(11)[:small]]),
+        jnp.stack([vec(4)[:small], vec(5)[:small]]),
         shares_attn[:, 3 * head_width :].T,
-        vec(5),
-        vec(4),
-        vec(2),
+        mid(5),
+        mid(4),
+        mid(2),
+        mid(3),
+        shares_mlp[:, :hidden],
         vec(3),
-        shares_mlp[:, :hidden],
-        vec(9),
         shares_mlp[:, hidden:].T,
-        vec(1),
-        vec(0),
+        mid(1),
+        mid(0),
     )
 
 

time: 632 us -> 373 us (0.59)
  waiting for transfers between devices: 219 us -> 19.2 us
  local copies, waits for them, and re-layouts: 44.1 us -> 18.7 us
  blocking collectives: 23.1 us -> 0 us
  between operations: 15.6 us -> 1.57 us
  other arithmetic: 19.5 us -> 6.09 us
  starting transfers between devices: 28.2 us -> 40 us
  Pallas kernels: 278 us -> 286 us
    reduce_scatter x2 -> x0, waiting for transfers between devices: 84.6 us -> none  [reduce_inner(): lax.psum_scatter(x, 'inner', scatter_dimension=0, tiled=True)]
    psum x1 -> x0, waiting for transfers between devices: 65.5 us -> none  [reduce_inner(): lax.psum(lax.psum_scatter(x, 'inner', scatter_dimension=0, tiled=True), '...]
    ppermute x30 -> x42, waiting for transfers between devices: 65.9 us -> 19.2 us  [the longest x3 6.39 us: groups(): lax.ppermute(total, 'outer', [(o, o ^ k) for o in range(self.outer_n)])]
    all_gather x1 -> x0, blocking collectives: 23.1 us -> none  [per_device(): lax.all_gather(jnp.concatenate([qv_bias.reshape(-1), fc1_bias]), 'tensor')]
    ppermute x30 -> x42, starting transfers between devices: 28 us -> 40 us  [the longest x10 17.5 us: over_z(): return lax.ppermute(x, 'tensor', [(i, i ^ k) for i in range(tensor_n)])]
    concatenate x20 -> x2, local copies, waits for them, and re-layouts: 10.5 us -> 0.15 us  [the longest x1 0.08 us: per_device(): jnp.concatenate([qv_bias[0], zeros[head_width:], zeros, qv_bias[1], ones,...]
    another operation x8 -> x6, other arithmetic: 9.92 us -> 0.59 us  [pair(): return jnp.stack([first, second])]
    slice x12 -> x7, local copies, waits for them, and re-layouts: 9.78 us -> 1.36 us  [the longest x1 0.72 us: per_device(): small_sums[:seq]]
  transfers between devices with their start and end apart: 34 -> 42, of which waited for: 13 -> 8; matrix products, arithmetic and copies ran while one was open for 6% -> 3% of each run, Pallas kernels for 24% -> 77%
where the time goes in v2:
time: 373 us; the launch traced here: 372 us
  Pallas kernels  286 us (77%)
  starting transfers between devices  40 us (11%)
  waiting for transfers between devices  19.2 us (5%)
  local copies, waits for them, and re-layouts  18.7 us (5%)
  other arithmetic  6.09 us (2%)
    pallas_call x4, Pallas kernels, attn_back(): pl.pallas_call(functools.partial(attn_back_kernel, heads=heads, tail_vali...  98.1 us
    pallas_call x4, Pallas kernels, mlp(): pl.pallas_call(functools.partial(mlp_kernel, gathered=gathered, accs=len(...  79.9 us
    pallas_call x5, Pallas kernels, attn(): pl.pallas_call(functools.partial(attn_kernel, heads=heads, tail_valid=tai...  72.5 us
    pallas_call x2, Pallas kernels, weight_grads(): pl.pallas_call(functools.partial(weight_grad_kernel, parts=parts), grid=(...  19.8 us
    ppermute x10, starting transfers between devices, over_z(): return lax.ppermute(x, 'tensor', [(i, i ^ k) for i in range(tensor_n)])  17.5 us
    pallas_call x1, Pallas kernels, enter(): pl.pallas_call(enter_kernel, grid=(crops,), in_specs=[whole(tok.shape), w...  9.24 us
    unnamed x79, local copies, waits for them, and re-layouts  8.17 us
  transfers between devices with their start and end apart: 42, of which 8 were waited for; matrix products, arithmetic and copies ran while one was open for 3% of the time, Pallas kernels for 77%

profile of v2, /device:TPU:0, one launch (start us, length us, event | category | flops | bytes accessed | tf_op | source)
XLA Modules:
  0.0 371.6 jit_solution(7203592183175339970)
XLA Ops:
  1.4 1.7 copy.51
  4.1 3.0 collective-permute-start
  7.1 2.6 collective-permute-start.1
  9.9 1.3 stack.110.vec_ref.refs_7_.refs_2_.refs_3_.refs_10_
  11.1 9.2 %enter.1 = (f32[8,272,768]{2,1,0:T(8,128)}, bf16[8,272,768]{2,1,0:T(8,128)(2,1)}) custom-call(bf16[261,8,768]{2,1,0:T(8,128)(2,1)} %bitcast.120, s32[8,256]{1,0:T(8,128)} %refs_9_.1, f32[9,768]{1,0:T(8,128)} %stack.110.vec_ref.refs_7_.refs_2_.refs_3_.refs_10_, f32[261,768]{1,0:T(8,128)} %pos_ref.1), custom_call_target="tpu_custom_call" | custom-call | flops 8049999872 | bytes 1048576 | tf_op jit(solution)/shard_map/enter/pallas_call | solution.py:148
  21.9 1.9 collective-permute-done.1
  23.9 1.5 collective-permute-start.2
  25.9 2.5 collective-permute-start.4
  28.4 9.4 %attention.5 = (f32[8,272,768]{2,1,0:T(8,128)}, bf16[8,272,768]{2,1,0:T(8,128)(2,1)}, f32[8,272,128]{2,1,0:T(8,128)}, bf16[1024,768]{1,0:T(8,128)(2,1)}, bf16[8,272,256]{2,1,0:T(8,128)(2,1)}) custom-call(bf16[8,272,768]{2,1,0:T(8,128)(2,1)} %get-tuple-element.138.refs_0_.refs_1_, f32[1,768]{1,0:T(1,128)} %copy-done.12, bf16[576,768]{1,0:T(8,128)(2,1)} %bitcast.97, ...), custom_call_target="tpu_custom_call" | custom-call | flops 9200000000 | bytes 1048576 | tf_op jit(solution)/shard_map/attention/pallas_call | solution.py:330
  37.9 1.6 collective-permute-start.6
  39.5 1.5 collective-permute-start.7
  41.0 6.6 %upstream.1.refs_1_.refs_2_ = bf16[8,272,768]{2,1,0:T(8,128)(2,1)} custom-call(bf16[261,8,768]{2,1,0:T(8,128)(2,1)} %bitcast.121), custom_call_target="tpu_custom_call" | custom-call | flops 6899999744 | bytes 1048576 | tf_op jit(solution)/shard_map/upstream/pallas_call | solution.py:168
  48.4 1.6 collective-permute-start.9
  50.0 1.5 collective-permute-start.10
  51.5 9.4 %attention.6 = (f32[8,272,768]{2,1,0:T(8,128)}, bf16[8,272,768]{2,1,0:T(8,128)(2,1)}, f32[8,272,128]{2,1,0:T(8,128)}, bf16[1024,768]{1,0:T(8,128)(2,1)}, bf16[8,272,256]{2,1,0:T(8,128)(2,1)}) custom-call(bf16[8,272,768]{2,1,0:T(8,128)(2,1)} %get-tuple-element.138.refs_0_.refs_1_, ...), custom_call_target="tpu_custom_call", output_to_operand_aliasing={{0}: (4, {}), {1}: (5, {}), {2}: (6, {}), {4}: (7, {})} | custom-call | flops 9200000000 | bytes 1048576 | tf_op jit(solution)/shard_map/attention/pallas_call | solution.py:330
  61.0 1.3 collective-permute-done.9.refs_3_
  62.3 1.6 collective-permute-start.13
  63.9 2.0 collective-permute-start.14
  65.9 16.4 %attention.7 = (f32[8,272,768]{2,1,0:T(8,128)}, bf16[8,272,768]{2,1,0:T(8,128)(2,1)}, f32[8,272,128]{2,1,0:T(8,128)}, bf16[1024,768]{1,0:T(8,128)(2,1)}) custom-call(s32[2]{0:T(128)} %pad_add_fusion.refs_0_.refs_6_, bf16[8,272,768]{2,1,0:T(8,128)(2,1)} %get-tuple-element.138.refs_0_.refs_1_, f32[2,104,768]{2,1,0:T(8,128)} %copy-done.8, ...), custom_call_target="tpu_custom_call" | custom-call | flops 18400000000 | bytes 1048576 | tf_op jit(solution)/shard_map/attention/pallas_call | solution.py:330
  83.7 1.3 collective-permute-start.17
  84.9 2.2 collective-permute-start.18
  87.1 16.5 %attention.8 = (f32[8,272,768]{2,1,0:T(8,128)}, bf16[8,272,768]{2,1,0:T(8,128)(2,1)}, f32[8,272,128]{2,1,0:T(8,128)}, bf16[1024,768]{1,0:T(8,128)(2,1)}) custom-call(s32[2]{0:T(128)} %pad_add_fusion.refs_0_.refs_6_, bf16[8,272,768]{2,1,0:T(8,128)(2,1)} %get-tuple-element.138.refs_0_.refs_1_, f32[2,104,768]{2,1,0:T(8,128)} %copy-done.7, ...), custom_call_target="tpu_custom_call" | custom-call | flops 18400000000 | bytes 1048576 | tf_op jit(solution)/shard_map/attention/pallas_call | solution.py:330
  103.9 1.2 collective-permute-start.20
  105.0 1.1 collective-permute-start.21
  106.2 1.4 collective-permute-start.23
  107.5 20.8 %attention.9 = (f32[8,272,768]{2,1,0:T(8,128)}, bf16[8,272,768]{2,1,0:T(8,128)(2,1)}, f32[8,272,128]{2,1,0:T(8,128)}, bf16[1024,768]{1,0:T(8,128)(2,1)}, bf16[8,272,768]{2,1,0:T(8,128)(2,1)}) custom-call(s32[2]{0:T(128)} %pad_add_fusion.refs_0_.refs_6_, bf16[8,272,768]{2,1,0:T(8,128)(2,1)} %get-tuple-element.138.refs_0_.refs_1_, f32[4,104,768]{2,1,0:T(8,128)} %copy-done.2, ...), custom_call_target="tpu_custom_call" | custom-call | flops 24149999616 | bytes 1048576 | tf_op jit(solution)/shard_map/attention/pallas_call | solution.py:330
  128.5 1.2 collective-permute-start.24
  129.7 2.5 collective-permute-start.25
  132.4 16.3 %mlp.4 = (f32[8,272,768]{2,1,0:T(8,128)}, f32[8,272,768]{2,1,0:T(8,128)}, bf16[8,272,768]{2,1,0:T(8,128)(2,1)}, bf16[8,272,768]{2,1,0:T(8,128)(2,1)}, bf16[8,272,768]{2,1,0:T(8,128)(2,1)}, /*index=5*/f32[8,768]{1,0:T(8,128)}) custom-call(bf16[8,272,768]{2,1,0:T(8,128)(2,1)} %get-tuple-element.162.refs_0_.refs_1_, ...), custom_call_target="tpu_custom_call" | custom-call | flops 19549999104 | bytes 1048576 | tf_op jit(solution)/shard_map/mlp/pallas_call | solution.py:643
  151.0 11.0 %weight_grads.2 = f32[768,1536]{1,0:T(8,128)} custom-call(bf16[2176,768]{1,0:T(8,128)(2,1)} %bitcast.124, bf16[2176,768]{1,0:T(8,128)(2,1)} %bitcast.127, bf16[2176,768]{1,0:T(8,128)(2,1)} %bitcast.128, bf16[2176,768]{1,0:T(8,128)(2,1)} %bitcast.126), custom_call_target="tpu_custom_call" | custom-call | flops 11500000256 | bytes 1048576 | tf_op jit(solution)/shard_map/weight_grads/pallas_call | solution.py:665
  162.2 3.7 dynamic-slice_bitcast_fusion
  165.9 1.1 collective-permute-start.30
  167.3 18.7 %mlp.5 = (f32[8,272,768]{2,1,0:T(8,128)}, f32[8,272,768]{2,1,0:T(8,128)}) custom-call(s32[2]{0:T(128)} %pad_add_fusion.refs_0_.refs_6_, bf16[8,272,768]{2,1,0:T(8,128)(2,1)} %get-tuple-element.162.refs_0_.refs_1_, bf16[8,272,768]{2,1,0:T(8,128)(2,1)} %upstream.1.refs_1_.refs_2_, f32[9,768]{1,0:T(8,128)} %stack.110.vec_ref.refs_7_.refs_2_.refs_3_.refs_10_, ...), custom_call_target="tpu_custom_call" | custom-call | flops 19549999104 | bytes 1048576 | tf_op jit(solution)/shard_map/mlp/pallas_call | solution.py:643
  187.3 1.4 bitcast_add_fusion.1
  189.7 16.4 %mlp.6 = (f32[8,272,768]{2,1,0:T(8,128)}, f32[8,272,768]{2,1,0:T(8,128)}) custom-call(s32[2]{0:T(128)} %pad_add_fusion.refs_0_.refs_6_, bf16[8,272,768]{2,1,0:T(8,128)(2,1)} %get-tuple-element.162.refs_0_.refs_1_, bf16[8,272,768]{2,1,0:T(8,128)(2,1)} %upstream.1.refs_1_.refs_2_, f32[9,768]{1,0:T(8,128)} %stack.110.vec_ref.refs_7_.refs_2_.refs_3_.refs_10_, ...), custom_call_target="tpu_custom_call" | custom-call | flops 19549999104 | bytes 1048576 | tf_op jit(solution)/shard_map/mlp/pallas_call | solution.py:643
  207.2 28.5 %mlp.7 = (bf16[261,8,768]{2,1,0:T(8,128)(2,1)}, f32[8,272,768]{2,1,0:T(8,128)}, bf16[8,272,768]{2,1,0:T(8,128)(2,1)}, f32[8,768]{1,0:T(8,128)}) custom-call(s32[2]{0:T(128)} %pad_add_fusion.refs_0_.refs_6_, bf16[8,272,768]{2,1,0:T(8,128)(2,1)} %get-tuple-element.162.refs_0_.refs_1_, bf16[8,272,768]{2,1,0:T(8,128)(2,1)} %upstream.1.refs_1_.refs_2_, ...), custom_call_target="tpu_custom_call" | custom-call | flops 32199999488 | bytes 1048576 | tf_op jit(solution)/shard_map/mlp/pallas_call | solution.py:643
  235.7 1.5 fusion
  237.2 1.2 collective-permute-start.35
  238.4 21.8 %attention_back.4 = (f32[8,272,768]{2,1,0:T(8,128)}, bf16[8,272,768]{2,1,0:T(8,128)(2,1)}, f32[8,256]{1,0:T(8,128)}) custom-call(bf16[8,272,768]{2,1,0:T(8,128)(2,1)} %get-tuple-element.187.refs_0_, bf16[1024,768]{1,0:T(8,128)(2,1)} %get-tuple-element.171.refs_1_, bf16[8,272,768]{2,1,0:T(8,128)(2,1)} %get-tuple-element.172.refs_2_, ...), custom_call_target="tpu_custom_call" | custom-call | flops 25300000768 | bytes 1048576 | tf_op jit(solution)/shard_map/attention_back/pallas_call | solution.py:486
  260.1 8.8 %weight_grads.3 = f32[768,768]{1,0:T(8,128)} custom-call(bf16[2176,768]{1,0:T(8,128)(2,1)} %bitcast.123, bf16[2176,768]{1,0:T(8,128)(2,1)} %bitcast.129, bf16[2176,768]{1,0:T(8,128)(2,1)} %bitcast.125, bf16[2176,256]{1,0:T(8,128)(2,1)} %bitcast.131), custom_call_target="tpu_custom_call" | custom-call | flops 11500000256 | bytes 1048576 | tf_op jit(solution)/shard_map/weight_grads/pallas_call | solution.py:665
  268.9 1.3 dynamic-slice_bitcast_fusion.1
  270.5 22.2 %attention_back.5.refs_5_ = f32[8,272,768]{2,1,0:T(8,128)} custom-call(bf16[8,272,768]{2,1,0:T(8,128)(2,1)} %get-tuple-element.187.refs_0_, bf16[1024,768]{1,0:T(8,128)(2,1)} %get-tuple-element.178.refs_1_, bf16[8,272,768]{2,1,0:T(8,128)(2,1)} %get-tuple-element.179.refs_2_, f32[8,272,128]{2,1,0:T(8,128)} %get-tuple-element.180.refs_3_, ...), custom_call_target="tpu_custom_call" | custom-call | flops 25300000768 | bytes 1048576 | tf_op jit(solution)/shard_map/attention_back/pallas_call | solution.py:486
  293.7 21.7 %attention_back.6.refs_4_ = f32[8,272,768]{2,1,0:T(8,128)} custom-call(bf16[8,272,768]{2,1,0:T(8,128)(2,1)} %get-tuple-element.187.refs_0_, bf16[1024,768]{1,0:T(8,128)(2,1)} %get-tuple-element.184.refs_1_, bf16[8,272,768]{2,1,0:T(8,128)(2,1)} %get-tuple-element.185.refs_2_, f32[8,272,128]{2,1,0:T(8,128)} %get-tuple-element.186.refs_3_), custom_call_target="tpu_custom_call" | custom-call | flops 25300000768 | bytes 1048576 | tf_op jit(solution)/shard_map/attention_back/pallas_call | solution.py:486
  315.6 1.2 collective-permute-start.38
  316.7 32.4 %attention_back.7 = (f32[2088,768]{1,0:T(8,128)}, f32[2,288,192]{2,1,0:T(8,128)}, f32[2,288,192]{2,1,0:T(8,128)}) custom-call(bf16[8,272,768]{2,1,0:T(8,128)(2,1)} %get-tuple-element.187.refs_0_, bf16[1024,768]{1,0:T(8,128)(2,1)} %get-tuple-element.188.refs_1_, bf16[8,272,768]{2,1,0:T(8,128)(2,1)} %get-tuple-element.189.refs_2_, ...), custom_call_target="tpu_custom_call" | custom-call | flops 35649998848 | bytes 1048576 | tf_op jit(solution)/shard_map/attention_back/pallas_call | solution.py:486
  350.2 2.0 collective-permute-done.39
  355.7 5.7 %collective-permute-done.40 = f32[288,192]{1,0:T(8,128)S(1)} collective-permute-done((f32[288,192]{1,0:T(8,128)S(1)}, f32[288,192]{1,0:T(8,128)S(1)}, u32[]{:S(2)}, u32[]{:S(2)}) %collective-permute-start.40) | collective-permute-done | bytes 221216 | tf_op jit(solution)/shard_map/ppermute | solution.py:711
  363.3 6.4 %collective-permute-done.41 = f32[288,192]{1,0:T(8,128)S(1)} collective-permute-done((f32[288,192]{1,0:T(8,128)S(1)}, f32[288,192]{1,0:T(8,128)S(1)}, u32[]{:S(2)}, u32[]{:S(2)}) %collective-permute-start.41) | collective-permute-done | bytes 221216 | tf_op jit(solution)/shard_map/ppermute | solution.py:718
  (189 shorter events, 22.4 us)
Async XLA Ops:
  4.1 17.9 %collective-permute-start = (f32[104,768]{1,0:T(8,128)S(1)}, f32[104,768]{1,0:T(8,128)S(1)}, u32[]{:S(2)}, u32[]{:S(2)}) collective-permute-start(f32[104,768]{1,0:T(8,128)S(1)} %get-tuple-element.251), channel_id=1, source_target_pairs={{0,8},{8,0},{16,24},{24,16},{1,9},{9,1},{17,25},{25,17},{2,10},{10... | collective-permute-start | bytes 958472 | tf_op jit(solution)/shard_map/ppermute | solution.py:782
  7.1 16.8 %collective-permute-start.1 = (f32[104,768]{1,0:T(8,128)S(1)}, f32[104,768]{1,0:T(8,128)S(1)}, u32[]{:S(2)}, u32[]{:S(2)}) collective-permute-start(f32[104,768]{1,0:T(8,128)S(1)} %get-tuple-element.251), channel_id=1, source_target_pairs={{0,16},{8,24},{16,0},{24,8},{1,17},{9,25},{17,1},{25,9},{2,18},{10... | collective-permute-start | bytes 958472 | tf_op jit(solution)/shard_map/ppermute | solution.py:782
  23.9 13.9 %collective-permute-start.2 = (f32[104,768]{1,0:T(8,128)S(1)}, f32[104,768]{1,0:T(8,128)S(1)}, u32[]{:S(2)}, u32[]{:S(2)}) collective-permute-start(f32[104,768]{1,0:T(8,128)S(1)} %collective-permute-done), channel_id=1, source_target_pairs={{0,4},{1,5},{2,3},{3,2},{4,0},{5,1},{6,7},{7,6},{8,12},{9,13},{10,... | collective-permute-start | bytes 958472 | tf_op jit(solution)/shard_map/ppermute | solution.py:819
  25.4 12.5 %collective-permute-start.3 = (f32[104,768]{1,0:T(8,128)S(1)}, f32[104,768]{1,0:T(8,128)S(1)}, u32[]{:S(2)}, u32[]{:S(2)}) collective-permute-start(f32[104,768]{1,0:T(8,128)S(1)} %collective-permute-done.1), channel_id=1, source_target_pairs={{0,4},{1,5},{2,3},{3,2},{4,0},{5,1},{6,7},{7,6},{8,12},{9,13},{10,... | collective-permute-start | bytes 958472 | tf_op jit(solution)/shard_map/ppermute | solution.py:819
  25.9 12.0 %collective-permute-start.4 = (f32[56,768]{1,0:T(8,128)S(1)}, f32[56,768]{1,0:T(8,128)S(1)}, u32[]{:S(2)}, u32[]{:S(2)}) collective-permute-start(f32[56,768]{1,0:T(8,128)S(1)} %slice.93), channel_id=1, source_target_pairs={{0,24},{8,16},{16,8},{24,0},{1,25},{9,17},{17,9},{25,1},{2,26},{10... | collective-permute-start | bytes 516104 | tf_op jit(solution)/shard_map/ppermute | solution.py:782
  28.4 9.5 %collective-permute-start.5 = (f32[104,768]{1,0:T(8,128)S(1)}, f32[104,768]{1,0:T(8,128)S(1)}, u32[]{:S(2)}, u32[]{:S(2)}) collective-permute-start(f32[104,768]{1,0:T(8,128)S(1)} %get-tuple-element.143), channel_id=1, source_target_pairs={{0,8},{8,0},{16,24},{24,16},{1,9},{9,1},{17,25},{25,17},{2,10},{10... | collective-permute-start | bytes 958472 | tf_op jit(solution)/shard_map/ppermute | solution.py:782
  37.9 10.5 %collective-permute-start.6 = (f32[2,104,768]{2,1,0:T(8,128)S(1)}, f32[2,104,768]{2,1,0:T(8,128)S(1)}, u32[]{:S(2)}, u32[]{:S(2)}) collective-permute-start(f32[2,104,768]{2,1,0:T(8,128)S(1)} %pad_maximum_fusion.4.refs_2_), channel_id=1, source_target_pairs={{0,1},{1,0},{2,6},{3,7},{4,5},{5,4},{6,2},{7,3},{8,9},{9,8},{10,14... | collective-permute-start | bytes 1916936 | tf_op jit(solution)/shard_map/ppermute | solution.py:829
  39.5 8.9 %collective-permute-start.8 = (f32[2,104,768]{2,1,0:T(8,128)S(1)}, f32[2,104,768]{2,1,0:T(8,128)S(1)}, u32[]{:S(2)}, u32[]{:S(2)}) collective-permute-start(f32[2,104,768]{2,1,0:T(8,128)S(1)} %pad_maximum_fusion.4.refs_2_), channel_id=1, source_target_pairs={{0,2},{1,3},{2,0},{3,1},{4,6},{5,7},{6,4},{7,5},{8,10},{9,11},{10,... | collective-permute-start | bytes 1916936 | tf_op jit(solution)/shard_map/ppermute | solution.py:829
  39.5 8.2 %collective-permute-start.7 = (f32[48,768]{1,0:T(8,128)S(1)}, f32[48,768]{1,0:T(8,128)S(1)}, u32[]{:S(2)}, u32[]{:S(2)}) collective-permute-start(f32[48,768]{1,0:T(8,128)S(1)} %slice.94), channel_id=1, source_target_pairs={{0,24},{8,16},{16,8},{24,0},{1,25},{9,17},{17,9},{25,1},{2,26},{10... | collective-permute-start | bytes 442376 | tf_op jit(solution)/shard_map/ppermute | solution.py:782
  48.4 13.9 %collective-permute-start.9 = (f32[2,104,768]{2,1,0:T(8,128)S(1)}, f32[2,104,768]{2,1,0:T(8,128)S(1)}, u32[]{:S(2)}, u32[]{:S(2)}) collective-permute-start(f32[2,104,768]{2,1,0:T(8,128)S(1)} %pad_maximum_fusion.5.refs_2_), channel_id=1, source_target_pairs={{0,1},{1,0},{2,6},{3,7},{4,5},{5,4},{6,2},{7,3},{8,9},{9,8},{10,14... | collective-permute-start | bytes 1916936 | tf_op jit(solution)/shard_map/ppermute | solution.py:836
  50.0 12.3 %collective-permute-start.12 = (f32[2,104,768]{2,1,0:T(8,128)S(1)}, f32[2,104,768]{2,1,0:T(8,128)S(1)}, u32[]{:S(2)}, u32[]{:S(2)}) collective-permute-start(f32[2,104,768]{2,1,0:T(8,128)S(1)} %pad_maximum_fusion.5.refs_2_), channel_id=1, source_target_pairs={{0,2},{1,3},{2,0},{3,1},{4,6},{5,7},{6,4},{7,5},{8,10},{9,11},{10,... | collective-permute-start | bytes 1916936 | tf_op jit(solution)/shard_map/ppermute | solution.py:836
  50.0 10.9 %collective-permute-start.10 = (f32[104,768]{1,0:T(8,128)S(1)}, f32[104,768]{1,0:T(8,128)S(1)}, u32[]{:S(2)}, u32[]{:S(2)}) collective-permute-start(f32[104,768]{1,0:T(8,128)S(1)} %pad_maximum_fusion.10), channel_id=1, source_target_pairs={{0,4},{1,5},{2,3},{3,2},{4,0},{5,1},{6,7},{7,6},{8,12},{9,13},{10,... | collective-permute-start | bytes 958472 | tf_op jit(solution)/shard_map/ppermute | solution.py:837
  51.5 10.8 %collective-permute-start.11 = (f32[2,104,768]{2,1,0:T(8,128)S(1)}, f32[2,104,768]{2,1,0:T(8,128)S(1)}, u32[]{:S(2)}, u32[]{:S(2)}) collective-permute-start(f32[2,104,768]{2,1,0:T(8,128)S(1)} %collective-permute-done.6.refs_3_), channel_id=1, source_target_pairs={{0,2},{1,3},{2,0},{3,1},{4,6},{5,7},{6,4},{7,5},{8,10},{9,11},{10,... | collective-permute-start | bytes 1916936 | tf_op jit(solution)/shard_map/ppermute | solution.py:835
  62.3 20.1 %collective-permute-start.13 = (f32[2,104,768]{2,1,0:T(8,128)S(1)}, f32[2,104,768]{2,1,0:T(8,128)S(1)}, u32[]{:S(2)}, u32[]{:S(2)}) collective-permute-start(f32[2,104,768]{2,1,0:T(8,128)S(1)} %pad_maximum_fusion.6), channel_id=1, source_target_pairs={{0,1},{1,0},{2,6},{3,7},{4,5},{5,4},{6,2},{7,3},{8,9},{9,8},{10,14... | collective-permute-start | bytes 1916936 | tf_op jit(solution)/shard_map/ppermute | solution.py:845
  63.9 18.5 %collective-permute-start.14 = (f32[96,768]{1,0:T(8,128)S(1)}, f32[96,768]{1,0:T(8,128)S(1)}, u32[]{:S(2)}, u32[]{:S(2)}) collective-permute-start(f32[96,768]{1,0:T(8,128)S(1)} %dynamic-slice_convert_fusion), channel_id=1, source_target_pairs={{0,8},{8,0},{16,24},{24,16},{1,9},{9,1},{17,25},{25,17},{2,10},{10... | collective-permute-start | bytes 884744 | tf_op jit(solution)/shard_map/ppermute | solution.py:782
  65.9 17.7 %collective-permute-start.15 = (f32[2,104,768]{2,1,0:T(8,128)S(1)}, f32[2,104,768]{2,1,0:T(8,128)S(1)}, u32[]{:S(2)}, u32[]{:S(2)}) collective-permute-start(f32[2,104,768]{2,1,0:T(8,128)S(1)} %collective-permute-done.9.refs_3_), channel_id=1, source_target_pairs={{0,2},{1,3},{2,0},{3,1},{4,6},{5,7},{6,4},{7,5},{8,10},{9,11},{10,... | collective-permute-start | bytes 1916936 | tf_op jit(solution)/shard_map/ppermute | solution.py:844
  65.9 17.7 %collective-permute-start.16 = (f32[104,768]{1,0:T(8,128)S(1)}, f32[104,768]{1,0:T(8,128)S(1)}, u32[]{:S(2)}, u32[]{:S(2)}) collective-permute-start(f32[104,768]{1,0:T(8,128)S(1)} %get-tuple-element.143), channel_id=1, source_target_pairs={{0,16},{8,24},{16,0},{24,8},{1,17},{9,25},{17,1},{25,9},{2,18},{10... | collective-permute-start | bytes 958472 | tf_op jit(solution)/shard_map/ppermute | solution.py:782
  82.6 21.0 %copy-start.2 = (f32[4,104,768]{2,1,0:T(8,128)}, f32[4,104,768]{2,1,0:T(8,128)S(1)}, u32[]{:S(2)}) copy-start(f32[4,104,768]{2,1,0:T(8,128)S(1)} %pad_maximum_fusion.refs_2_) | copy-start | bytes 3833860
  83.7 20.0 %collective-permute-start.17 = (f32[200,768]{1,0:T(8,128)S(1)}, f32[200,768]{1,0:T(8,128)S(1)}, u32[]{:S(2)}, u32[]{:S(2)}) collective-permute-start(f32[200,768]{1,0:T(8,128)S(1)} %pad_maximum_fusion.7), channel_id=1, source_target_pairs={{0,4},{1,5},{2,3},{3,2},{4,0},{5,1},{6,7},{7,6},{8,12},{9,13},{10,... | collective-permute-start | bytes 1843208 | tf_op jit(solution)/shard_map/ppermute | solution.py:853
  84.9 18.7 %collective-permute-start.18 = (f32[96,768]{1,0:T(8,128)S(1)}, f32[96,768]{1,0:T(8,128)S(1)}, u32[]{:S(2)}, u32[]{:S(2)}) collective-permute-start(f32[96,768]{1,0:T(8,128)S(1)} %dynamic-slice_convert_fusion), channel_id=1, source_target_pairs={{0,16},{8,24},{16,0},{24,8},{1,17},{9,25},{17,1},{25,9},{2,18},{10... | collective-permute-start | bytes 884744 | tf_op jit(solution)/shard_map/ppermute | solution.py:782
  87.1 16.7 %collective-permute-start.19 = (f32[4,104,768]{2,1,0:T(8,128)S(1)}, f32[4,104,768]{2,1,0:T(8,128)S(1)}, u32[]{:S(2)}, u32[]{:S(2)}) collective-permute-start(f32[4,104,768]{2,1,0:T(8,128)S(1)} %pad_maximum_fusion.refs_2_), channel_id=1, source_target_pairs={{0,2},{1,3},{2,0},{3,1},{4,6},{5,7},{6,4},{7,5},{8,10},{9,11},{10,... | collective-permute-start | bytes 3833864 | tf_op jit(solution)/shard_map/ppermute | solution.py:852
  103.8 24.5 %copy-start.3 = (f32[2,200,768]{2,1,0:T(8,128)}, f32[2,200,768]{2,1,0:T(8,128)S(1)}, u32[]{:S(2)}) copy-start(f32[2,200,768]{2,1,0:T(8,128)S(1)} %pad_maximum_fusion.1.refs_4_) | copy-start | bytes 3686404
  103.9 24.6 %collective-permute-start.20 = (f32[2,200,768]{2,1,0:T(8,128)S(1)}, f32[2,200,768]{2,1,0:T(8,128)S(1)}, u32[]{:S(2)}, u32[]{:S(2)}) collective-permute-start(f32[2,200,768]{2,1,0:T(8,128)S(1)} %pad_maximum_fusion.1.refs_4_), channel_id=1, source_target_pairs={{0,1},{1,0},{2,6},{3,7},{4,5},{5,4},{6,2},{7,3},{8,9},{9,8},{10,14... | collective-permute-start | bytes 3686408 | tf_op jit(solution)/shard_map/ppermute | solution.py:859
  105.0 23.5 %collective-permute-start.22 = (f32[2,200,768]{2,1,0:T(8,128)S(1)}, f32[2,200,768]{2,1,0:T(8,128)}, u32[]{:S(2)}, u32[]{:S(2)}) collective-permute-start(f32[2,200,768]{2,1,0:T(8,128)S(1)} %pad_maximum_fusion.1.refs_4_), channel_id=1, source_target_pairs={{0,2},{1,3},{2,0},{3,1},{4,6},{5,7},{6,4},{7,5},{8,10},{9,11},{10,... | collective-permute-start | bytes 3686408 | tf_op jit(solution)/shard_map/ppermute | solution.py:859
  105.0 23.3 %collective-permute-start.21 = (f32[200,768]{1,0:T(8,128)S(1)}, f32[200,768]{1,0:T(8,128)S(1)}, u32[]{:S(2)}, u32[]{:S(2)}) collective-permute-start(f32[200,768]{1,0:T(8,128)S(1)} %pad_maximum_fusion.8), channel_id=1, source_target_pairs={{0,4},{1,5},{2,3},{3,2},{4,0},{5,1},{6,7},{7,6},{8,12},{9,13},{10,... | collective-permute-start | bytes 1843208 | tf_op jit(solution)/shard_map/ppermute | solution.py:860
  106.2 22.3 %collective-permute-start.23 = (f32[104,768]{1,0:T(8,128)S(1)}, f32[104,768]{1,0:T(8,128)S(1)}, u32[]{:S(2)}, u32[]{:S(2)}) collective-permute-start(f32[104,768]{1,0:T(8,128)S(1)} %get-tuple-element.143), channel_id=1, source_target_pairs={{0,24},{8,16},{16,8},{24,0},{1,25},{9,17},{17,9},{25,1},{2,26},{10... | collective-permute-start | bytes 958472 | tf_op jit(solution)/shard_map/ppermute | solution.py:782
  128.4 20.2 %copy-start.4 = (f32[2,200,768]{2,1,0:T(8,128)}, f32[2,200,768]{2,1,0:T(8,128)S(1)}, u32[]{:S(2)}) copy-start(f32[2,200,768]{2,1,0:T(8,128)S(1)} %pad_maximum_fusion.2.refs_4_) | copy-start | bytes 3686404
  128.5 20.2 %copy-start.24 = (f32[2,200,768]{2,1,0:T(8,128)}, f32[2,200,768]{2,1,0:T(8,128)S(1)}, u32[]{:S(2)}) copy-start(f32[2,200,768]{2,1,0:T(8,128)S(1)} %collective-permute-done.20.refs_5_) | copy-start | bytes 3686404
  128.5 20.2 %collective-permute-start.24 = (f32[2,200,768]{2,1,0:T(8,128)S(1)}, f32[2,200,768]{2,1,0:T(8,128)}, u32[]{:S(2)}, u32[]{:S(2)}) collective-permute-start(f32[2,200,768]{2,1,0:T(8,128)S(1)} %pad_maximum_fusion.2.refs_4_), channel_id=1, source_target_pairs={{0,1},{1,0},{2,6},{3,7},{4,5},{5,4},{6,2},{7,3},{8,9},{9,8},{10,14... | collective-permute-start | bytes 3686408 | tf_op jit(solution)/shard_map/ppermute | solution.py:867
  129.7 19.1 %collective-permute-start.27 = (f32[2,200,768]{2,1,0:T(8,128)S(1)}, f32[2,200,768]{2,1,0:T(8,128)S(1)}, u32[]{:S(2)}, u32[]{:S(2)}) collective-permute-start(f32[2,200,768]{2,1,0:T(8,128)S(1)} %pad_maximum_fusion.2.refs_4_), channel_id=1, source_target_pairs={{0,2},{1,3},{2,0},{3,1},{4,6},{5,7},{6,4},{7,5},{8,10},{9,11},{10,... | collective-permute-start | bytes 3686408 | tf_op jit(solution)/shard_map/ppermute | solution.py:867
  129.7 19.0 %collective-permute-start.25 = (f32[96,768]{1,0:T(8,128)S(1)}, f32[96,768]{1,0:T(8,128)S(1)}, u32[]{:S(2)}, u32[]{:S(2)}) collective-permute-start(f32[96,768]{1,0:T(8,128)S(1)} %dynamic-slice_convert_fusion), channel_id=1, source_target_pairs={{0,24},{8,16},{16,8},{24,0},{1,25},{9,17},{17,9},{25,1},{2,26},{10... | collective-permute-start | bytes 884744 | tf_op jit(solution)/shard_map/ppermute | solution.py:782
  132.1 16.6 %collective-permute-start.26 = (f32[2,200,768]{2,1,0:T(8,128)S(1)}, f32[2,200,768]{2,1,0:T(8,128)S(1)}, u32[]{:S(2)}, u32[]{:S(2)}) collective-permute-start(f32[2,200,768]{2,1,0:T(8,128)S(1)} %collective-permute-done.20.refs_5_), channel_id=1, source_target_pairs={{0,2},{1,3},{2,0},{3,1},{4,6},{5,7},{6,4},{7,5},{8,10},{9,11},{10,... | collective-permute-start | bytes 3686408 | tf_op jit(solution)/shard_map/ppermute | solution.py:866
  149.9 12.3 %collective-permute-start.29 = (f32[2,200,768]{2,1,0:T(8,128)}, f32[2,200,768]{2,1,0:T(8,128)}, u32[]{:S(2)}, u32[]{:S(2)}) collective-permute-start(f32[2,200,768]{2,1,0:T(8,128)} %collective-permute-done.24.refs_5_), channel_id=1, source_target_pairs={{0,2},{1,3},{2,0},{3,1},{4,6},{5,7},{6,4},{7,5},{8,10},{9,11},{10,... | collective-permute-start | bytes 3686408 | tf_op jit(solution)/shard_map/ppermute | solution.py:876
  150.2 11.8 %collective-permute-start.28 = (f32[200,768]{1,0:T(8,128)S(1)}, f32[200,768]{1,0:T(8,128)S(1)}, u32[]{:S(2)}, u32[]{:S(2)}) collective-permute-start(f32[200,768]{1,0:T(8,128)S(1)} %pad_maximum_fusion.9), channel_id=1, source_target_pairs={{0,4},{1,5},{2,3},{3,2},{4,0},{5,1},{6,7},{7,6},{8,12},{9,13},{10,... | collective-permute-start | bytes 1843208 | tf_op jit(solution)/shard_map/ppermute | solution.py:877
  162.1 25.1 %slice-start = ((s8[4718592]{0:T(1024)(128)(4,1)}), s8[524288]{0:T(1024)(128)(4,1)S(1)}, s32[]{:S(2)}) async-start(s8[4718592]{0:T(1024)(128)(4,1)} %bitcast.84), calls=%async_computation | async-start | bytes 1048576
  165.8 20.2 %collective-permute-start.32 = (f32[2,192,1536]{2,1,0:T(8,128)}, f32[2,192,1536]{2,1,0:T(8,128)}, u32[]{:S(2)}, u32[]{:S(2)}) collective-permute-start(f32[2,192,1536]{2,1,0:T(8,128)} %dynamic-slice_bitcast_fusion), channel_id=1, source_target_pairs={{0,2},{2,0},{4,6},{6,4},{1,3},{3,1},{5,7},{7,5},{8,10},{10,8},{12,... | collective-permute-start | bytes 7077896 | tf_op jit(solution)/shard_map/ppermute | solution.py:701
  165.9 20.1 %collective-permute-start.30 = (f32[2,200,768]{2,1,0:T(8,128)S(1)}, f32[2,200,768]{2,1,0:T(8,128)}, u32[]{:S(2)}, u32[]{:S(2)}) collective-permute-start(f32[2,200,768]{2,1,0:T(8,128)S(1)} %pad_maximum_fusion.3.refs_4_), channel_id=1, source_target_pairs={{0,1},{1,0},{2,6},{3,7},{4,5},{5,4},{6,2},{7,3},{8,9},{9,8},{10,14... | collective-permute-start | bytes 3686408 | tf_op jit(solution)/shard_map/ppermute | solution.py:886
  167.0 19.0 %collective-permute-start.31 = (f32[2,200,768]{2,1,0:T(8,128)S(1)}, f32[2,200,768]{2,1,0:T(8,128)S(1)}, u32[]{:S(2)}, u32[]{:S(2)}) collective-permute-start(f32[2,200,768]{2,1,0:T(8,128)S(1)} %pad_maximum_fusion.3.refs_4_), channel_id=1, source_target_pairs={{0,2},{1,3},{2,0},{3,1},{4,6},{5,7},{6,4},{7,5},{8,10},{9,11},{10,... | collective-permute-start | bytes 3686408 | tf_op jit(solution)/shard_map/ppermute | solution.py:886
  187.1 19.1 %collective-permute-start.33 = (f32[2,200,768]{2,1,0:T(8,128)}, f32[2,200,768]{2,1,0:T(8,128)S(1)}, u32[]{:S(2)}, u32[]{:S(2)}) collective-permute-start(f32[2,200,768]{2,1,0:T(8,128)} %collective-permute-done.30.refs_5_), channel_id=1, source_target_pairs={{0,2},{1,3},{2,0},{3,1},{4,6},{5,7},{6,4},{7,5},{8,10},{9,11},{10,... | collective-permute-start | bytes 3686408 | tf_op jit(solution)/shard_map/ppermute | solution.py:891
  188.7 47.0 %collective-permute-start.34 = (f32[192,1536]{1,0:T(8,128)S(1)}, f32[192,1536]{1,0:T(8,128)S(1)}, u32[]{:S(2)}, u32[]{:S(2)}) collective-permute-start(f32[192,1536]{1,0:T(8,128)S(1)} %bitcast_add_fusion.1), channel_id=1, source_target_pairs={{0,4},{2,6},{4,0},{6,2},{1,5},{3,7},{5,1},{7,3},{8,12},{10,14},{12... | collective-permute-start | bytes 3538952 | tf_op jit(solution)/shard_map/ppermute | solution.py:711
  237.2 33.2 %collective-permute-start.35 = (f32[192,1536]{1,0:T(8,128)S(1)}, f32[192,1536]{1,0:T(8,128)S(1)}, u32[]{:S(2)}, u32[]{:S(2)}) collective-permute-start(f32[192,1536]{1,0:T(8,128)S(1)} %fusion), channel_id=1, source_target_pairs={{0,1},{1,0},{2,3},{3,2},{4,5},{5,4},{6,7},{7,6},{8,9},{9,8},{10,11... | collective-permute-start | bytes 3538952 | tf_op jit(solution)/shard_map/ppermute | solution.py:718
  270.3 22.4 %collective-permute-start.36 = (f32[2,192,768]{2,1,0:T(8,128)S(1)}, f32[2,192,768]{2,1,0:T(8,128)S(1)}, u32[]{:S(2)}, u32[]{:S(2)}) collective-permute-start(f32[2,192,768]{2,1,0:T(8,128)S(1)} %dynamic-slice_bitcast_fusion.1), channel_id=1, source_target_pairs={{0,2},{2,0},{4,6},{6,4},{1,3},{3,1},{5,7},{7,5},{8,10},{10,8},{12,... | collective-permute-start | bytes 3538952 | tf_op jit(solution)/shard_map/ppermute | solution.py:701
  270.5 22.2 %copy-start = (f32[768,768]{1,0:T(8,128)S(1)}, f32[768,768]{1,0:T(8,128)}, u32[]{:S(2)}) copy-start(f32[768,768]{1,0:T(8,128)} %weight_grads.3) | copy-start | bytes 7077892
  292.8 22.7 %collective-permute-start.37 = (f32[192,768]{1,0:T(8,128)S(1)}, f32[192,768]{1,0:T(8,128)S(1)}, u32[]{:S(2)}, u32[]{:S(2)}) collective-permute-start(f32[192,768]{1,0:T(8,128)S(1)} %bitcast_add_fusion.3), channel_id=1, source_target_pairs={{0,4},{2,6},{4,0},{6,2},{1,5},{3,7},{5,1},{7,3},{8,12},{10,14},{12... | collective-permute-start | bytes 1769480 | tf_op jit(solution)/shard_map/ppermute | solution.py:711
  315.6 33.6 %collective-permute-start.38 = (f32[192,768]{1,0:T(8,128)S(1)}, f32[192,768]{1,0:T(8,128)S(1)}, u32[]{:S(2)}, u32[]{:S(2)}) collective-permute-start(f32[192,768]{1,0:T(8,128)S(1)} %fusion.1), channel_id=1, source_target_pairs={{0,1},{1,0},{2,3},{3,2},{4,5},{5,4},{6,7},{7,6},{8,9},{9,8},{10,11... | collective-permute-start | bytes 1769480 | tf_op jit(solution)/shard_map/ppermute | solution.py:718
  350.2 2.0 collective-permute-start.39
  352.2 9.1 %collective-permute-start.40 = (f32[288,192]{1,0:T(8,128)S(1)}, f32[288,192]{1,0:T(8,128)S(1)}, u32[]{:S(2)}, u32[]{:S(2)}) collective-permute-start(f32[288,192]{1,0:T(8,128)S(1)} %add_bitcast_fusion), channel_id=1, source_target_pairs={{0,4},{2,6},{4,0},{6,2},{1,5},{3,7},{5,1},{7,3},{8,12},{10,14},{12... | collective-permute-start | bytes 663560 | tf_op jit(solution)/shard_map/ppermute | solution.py:711
  361.4 8.3 %collective-permute-start.41 = (f32[288,192]{1,0:T(8,128)S(1)}, f32[288,192]{1,0:T(8,128)S(1)}, u32[]{:S(2)}, u32[]{:S(2)}) collective-permute-start(f32[288,192]{1,0:T(8,128)S(1)} %bitcast_add_fusion.4), channel_id=1, source_target_pairs={{0,1},{1,0},{2,3},{3,2},{4,5},{5,4},{6,7},{7,6},{8,9},{9,8},{10,11... | collective-permute-start | bytes 663560 | tf_op jit(solution)/shard_map/ppermute | solution.py:718
  (32 other events, 209.9 us)
